TPU v7x, 32 devices: a whole 2x2x4 slice. The times are simulated.
32 devices in a mesh: row: 4 (over z), col: 8 (over y, x, core).
Axes of the slice: x: 2, y: 2, z: 4, core: 2. Of those that a mesh axis runs over, the one named last changes fastest.
Arguments:
- factor: bfloat16 [16, 4, 8, 8, 128, 128], P(None, 'row', None, 'col'), may hold values from -0.09375 to 0.09375
- pattern: int32 [16, 4, 8, 8], P(None, 'row', None, 'col'), may hold values 0 or 1
- loads: float32 [8, 8, 128, 256], P(None, 'col'), may hold values from -6 to 6
- block_inverse: float32 [8, 8, 128, 128], P(None, 'col'), may hold values from -1 to 2, as said below
Outputs:
- solution: float32 [8, 8, 128, 256], P(None, 'col')
Inputs may be any that keep to these rules, and one draw needn't show every extreme that they name: `block_inverse`: each block is lower triangular with diagonal entries between 0.5 and 1.5.
All inputs are finite; a program needn't handle non-finite values. No bound on the sum of `pattern` on one device may be relied on, other than what follows from the above.
Results may differ from a plain program's by a relative error of at most 0.0045.
Values may be sent and summed in bfloat16 or wider, within the bound.
A program may use at most 128 MiB of HBM per device.

v0:
```python
import jax
import jax.numpy as jnp
from jax import lax
from jax.sharding import PartitionSpec as P

LEVELS = 8


def spread(value, axis, source):
    kept = jnp.where(lax.axis_index(axis) == source, value, 0).astype(value.dtype)
    return lax.psum(kept, axis)


def per_device(factor, pattern, loads, block_inverse):
    row_count = lax.axis_size("row")
    col_count = lax.axis_size("col")
    groups = col_count // row_count
    my_row = lax.axis_index("row")
    my_col = lax.axis_index("col")
    masked = factor[:, 0, :, 0] * pattern[:, 0, :, 0].astype(jnp.bfloat16)[:, :, None, None]
    per_row = factor.shape[0] // LEVELS
    per_col = factor.shape[2] // LEVELS
    rhs_local = loads[:, 0]
    inverse_local = block_inverse[:, 0]
    forward_vals = []
    forward_low = []
    for level_id in range(LEVELS):
        rhs_level = rhs_local[level_id * per_col : (level_id + 1) * per_col]
        inverse_level = inverse_local[level_id * per_col : (level_id + 1) * per_col]
        if level_id > 0:
            panel = masked[level_id * per_row : (level_id + 1) * per_row, : level_id * per_col]
            earlier = jnp.concatenate(forward_low, axis=0)
            partial_sum = jnp.einsum(
                "abpq,bqs->aps", panel, earlier, preferred_element_type=jnp.float32
            )
            row_total = lax.psum(partial_sum, "col")
            row_total = row_total.reshape((per_col, groups) + row_total.shape[1:])
            own_total = lax.dynamic_index_in_dim(
                row_total, my_col // row_count, axis=1, keepdims=False
            )
            solved = jnp.einsum(
                "mpq,mqs->mps",
                inverse_level,
                rhs_level - own_total,
                precision=lax.Precision.HIGHEST,
            )
            solved = spread(solved, "row", my_col % row_count)
        else:
            solved = jnp.einsum(
                "mpq,mqs->mps", inverse_level, rhs_level, precision=lax.Precision.HIGHEST
            )
        forward_vals.append(solved)
        forward_low.append(solved.astype(jnp.bfloat16))
    solution_parts = [None] * LEVELS
    later = []
    for level_id in reversed(range(LEVELS)):
        inverse_level = inverse_local[level_id * per_col : (level_id + 1) * per_col]
        resid = forward_vals[level_id]
        if level_id < LEVELS - 1:
            panel = masked[
                (level_id + 1) * per_row :, level_id * per_col : (level_id + 1) * per_col
            ]
            after = jnp.concatenate(later, axis=0)
            partial_sum = jnp.einsum(
                "abpq,aps->bqs", panel, after, preferred_element_type=jnp.float32
            )
            resid = resid - lax.psum(partial_sum, "row")
        solved = jnp.einsum("mqp,mqs->mps", inverse_level, resid, precision=lax.Precision.HIGHEST)
        solution_parts[level_id] = solved
        if level_id > 0:
            low_solved = solved.astype(jnp.bfloat16)
            pieces = lax.all_gather(low_solved[None], "col", axis=0, tiled=True)
            pieces = pieces.reshape((groups, row_count) + low_solved.shape)
            picked = lax.dynamic_index_in_dim(pieces, my_row, axis=1, keepdims=False)
            arranged = jnp.swapaxes(picked, 0, 1).reshape((per_row,) + low_solved.shape[1:])
            later = [arranged] + later
    solution = jnp.concatenate(solution_parts, axis=0)
    return solution[:, None]


def solution(mesh):
    in_specs = (
        P(None, "row", None, "col", None, None),
        P(None, "row", None, "col"),
        P(None, "col", None, None),
        P(None, "col", None, None),
    )
    out_specs = P(None, "col", None, None)
    return jax.shard_map(
        per_device, mesh=mesh, in_specs=in_specs, out_specs=out_specs, check_vma=False
    )
```

profile of v0, /device:TPU:0, one launch (start us, length us, event | category | flops | bytes accessed | tf_op | source)
XLA Modules:
  0.0 1002.7 jit_solution(2434876398146998311)
XLA Ops:
  14.0 56.3 %all-reduce.22.cloned.1.call-done = f32[2,128,256]{2,1,0:T(8,128)} async-done(((f32[2,128,256]{2,1,0:T(8,128)}), f32[2,128,256]{2,1,0:T(8,128)}) %all-reduce.22.cloned.1.call-update) | async-done | bytes 262160 | tf_op jit(solution)/shard_map/psum | solution.py:36
  72.2 34.3 %all-reduce.24.cloned.1.call-done = f32[1,128,256]{2,1,0:T(8,128)} async-done(((f32[1,128,256]{2,1,0:T(8,128)}), f32[1,128,256]{2,1,0:T(8,128)}) %all-reduce.24.cloned.1.call-update) | async-done | bytes 131088 | tf_op jit(solution)/shard_map/psum | solution.py:11
  109.4 53.5 %all-reduce.26.cloned.1.call-done = f32[2,128,256]{2,1,0:T(8,128)} async-done(((f32[2,128,256]{2,1,0:T(8,128)}), f32[2,128,256]{2,1,0:T(8,128)}) %all-reduce.26.cloned.1.call-update) | async-done | bytes 262160 | tf_op jit(solution)/shard_map/psum | solution.py:36
  164.8 34.2 %all-reduce.28.cloned.1.call-done = f32[1,128,256]{2,1,0:T(8,128)} async-done(((f32[1,128,256]{2,1,0:T(8,128)}), f32[1,128,256]{2,1,0:T(8,128)}) %all-reduce.28.cloned.1.call-update) | async-done | bytes 131088 | tf_op jit(solution)/shard_map/psum | solution.py:11
  201.9 53.3 %all-reduce.30.cloned.1.call-done = f32[2,128,256]{2,1,0:T(8,128)} async-done(((f32[2,128,256]{2,1,0:T(8,128)}), f32[2,128,256]{2,1,0:T(8,128)}) %all-reduce.30.cloned.1.call-update) | async-done | bytes 262160 | tf_op jit(solution)/shard_map/psum | solution.py:36
  257.1 34.3 %all-reduce.32.cloned.1.call-done = f32[1,128,256]{2,1,0:T(8,128)} async-done(((f32[1,128,256]{2,1,0:T(8,128)}), f32[1,128,256]{2,1,0:T(8,128)}) %all-reduce.32.cloned.1.call-update) | async-done | bytes 131088 | tf_op jit(solution)/shard_map/psum | solution.py:11
  294.3 53.4 %all-reduce.34.cloned.1.call-done = f32[2,128,256]{2,1,0:T(8,128)} async-done(((f32[2,128,256]{2,1,0:T(8,128)}), f32[2,128,256]{2,1,0:T(8,128)}) %all-reduce.34.cloned.1.call-update) | async-done | bytes 262160 | tf_op jit(solution)/shard_map/psum | solution.py:36
  349.6 34.3 %all-reduce.36.cloned.1.call-done = f32[1,128,256]{2,1,0:T(8,128)} async-done(((f32[1,128,256]{2,1,0:T(8,128)}), f32[1,128,256]{2,1,0:T(8,128)}) %all-reduce.36.cloned.1.call-update) | async-done | bytes 131088 | tf_op jit(solution)/shard_map/psum | solution.py:11
  386.8 53.3 %all-reduce.38.cloned.1.call-done = f32[2,128,256]{2,1,0:T(8,128)} async-done(((f32[2,128,256]{2,1,0:T(8,128)}), f32[2,128,256]{2,1,0:T(8,128)}) %all-reduce.38.cloned.1.call-update) | async-done | bytes 262160 | tf_op jit(solution)/shard_map/psum | solution.py:36
  442.1 34.2 %all-reduce.40.cloned.1.call-done = f32[1,128,256]{2,1,0:T(8,128)} async-done(((f32[1,128,256]{2,1,0:T(8,128)}), f32[1,128,256]{2,1,0:T(8,128)}) %all-reduce.40.cloned.1.call-update) | async-done | bytes 131088 | tf_op jit(solution)/shard_map/psum | solution.py:11
  479.3 53.3 %all-reduce.42.cloned.1.call-done = f32[2,128,256]{2,1,0:T(8,128)} async-done(((f32[2,128,256]{2,1,0:T(8,128)}), f32[2,128,256]{2,1,0:T(8,128)}) %all-reduce.42.cloned.1.call-update) | async-done | bytes 262160 | tf_op jit(solution)/shard_map/psum | solution.py:36
  534.5 34.2 %all-reduce.44.cloned.1.call-done = f32[1,128,256]{2,1,0:T(8,128)} async-done(((f32[1,128,256]{2,1,0:T(8,128)}), f32[1,128,256]{2,1,0:T(8,128)}) %all-reduce.44.cloned.1.call-update) | async-done | bytes 131088 | tf_op jit(solution)/shard_map/psum | solution.py:11
  571.8 53.3 %all-reduce.46.cloned.1.call-done = f32[2,128,256]{2,1,0:T(8,128)} async-done(((f32[2,128,256]{2,1,0:T(8,128)}), f32[2,128,256]{2,1,0:T(8,128)}) %all-reduce.46.cloned.1.call-update) | async-done | bytes 262160 | tf_op jit(solution)/shard_map/psum | solution.py:36
  627.0 34.2 %all-reduce.48.cloned.1.call-done = f32[128,256]{1,0:T(8,128)} async-done(((f32[128,256]{1,0:T(8,128)}), f32[128,256]{1,0:T(8,128)}) %all-reduce.48.cloned.1.call-update) | async-done | bytes 131088 | tf_op jit(solution)/shard_map/psum | solution.py:11
  675.0 33.4 %all-reduce.50.cloned.1.call-done = f32[1,128,256]{2,1,0:T(8,128)} async-done(((f32[1,128,256]{2,1,0:T(8,128)}), f32[1,128,256]{2,1,0:T(8,128)}) %all-reduce.50.cloned.1.call-update) | async-done | bytes 131088 | tf_op jit(solution)/shard_map/psum | solution.py:67
  722.3 33.3 %all-reduce.52.cloned.1.call-done = f32[1,128,256]{2,1,0:T(8,128)} async-done(((f32[1,128,256]{2,1,0:T(8,128)}), f32[1,128,256]{2,1,0:T(8,128)}) %all-reduce.52.cloned.1.call-update) | async-done | bytes 131088 | tf_op jit(solution)/shard_map/psum | solution.py:67
  756.9 9.9 all-gather.2
  769.6 33.4 %all-reduce.54.cloned.1.call-done = f32[1,128,256]{2,1,0:T(8,128)} async-done(((f32[1,128,256]{2,1,0:T(8,128)}), f32[1,128,256]{2,1,0:T(8,128)}) %all-reduce.54.cloned.1.call-update) | async-done | bytes 131088 | tf_op jit(solution)/shard_map/psum | solution.py:67
  816.9 33.3 %all-reduce.56.cloned.1.call-done = f32[1,128,256]{2,1,0:T(8,128)} async-done(((f32[1,128,256]{2,1,0:T(8,128)}), f32[1,128,256]{2,1,0:T(8,128)}) %all-reduce.56.cloned.1.call-update) | async-done | bytes 131088 | tf_op jit(solution)/shard_map/psum | solution.py:67
  851.5 10.1 %all-gather.4 = bf16[1024,256]{0,1:T(8,128)(2,1)S(1)} all-gather(bf16[128,256]{0,1:T(8,128)(2,1)S(1)} %get-tuple-element.34), channel_id=6, replica_groups=mesh['row'=4,'col'=8] {'col'}, dimensions={0}, use_global_device_ids=true | all-gather | bytes 589824 | tf_op jit(solution)/shard_map/all_gather | solution.py:72
  864.5 33.4 %all-reduce.58.cloned.1.call-done = f32[1,128,256]{2,1,0:T(8,128)} async-done(((f32[1,128,256]{2,1,0:T(8,128)}), f32[1,128,256]{2,1,0:T(8,128)}) %all-reduce.58.cloned.1.call-update) | async-done | bytes 131088 | tf_op jit(solution)/shard_map/psum | solution.py:67
  912.1 33.3 %all-reduce.60.cloned.1.call-done = f32[1,128,256]{2,1,0:T(8,128)} async-done(((f32[1,128,256]{2,1,0:T(8,128)}), f32[1,128,256]{2,1,0:T(8,128)}) %all-reduce.60.cloned.1.call-update) | async-done | bytes 131088 | tf_op jit(solution)/shard_map/psum | solution.py:67
  946.7 9.9 all-gather.6
  959.6 33.5 %all-reduce.62.cloned.1.call-done = f32[1,128,256]{2,1,0:T(8,128)} async-done(((f32[1,128,256]{2,1,0:T(8,128)}), f32[1,128,256]{2,1,0:T(8,128)}) %all-reduce.62.cloned.1.call-update) | async-done | bytes 131088 | tf_op jit(solution)/shard_map/psum | solution.py:67
  (154 shorter events, 108.6 us)
Async XLA Ops:
  6.5 63.8 %all-reduce.22.cloned.1.call-start = ((), (), s32[]{:S(2)}) async-start(), calls=%async_computation | async-start | bytes 524288 | tf_op jit(solution)/shard_map/psum | solution.py:36
  14.0 92.6 %all-reduce.24.cloned.1.call-start = ((), (), s32[]{:S(2)}) async-start(), calls=%async_computation.1 | async-start | bytes 262144 | tf_op jit(solution)/shard_map/psum | solution.py:11
  72.2 90.7 %all-reduce.26.cloned.1.call-start = ((), (), s32[]{:S(2)}) async-start(), calls=%async_computation.2 | async-start | bytes 524288 | tf_op jit(solution)/shard_map/psum | solution.py:36
  109.3 89.7 %all-reduce.28.cloned.1.call-start = ((), (), s32[]{:S(2)}) async-start(), calls=%async_computation.3 | async-start | bytes 262144 | tf_op jit(solution)/shard_map/psum | solution.py:11
  164.7 90.5 %all-reduce.30.cloned.1.call-start = ((), (), s32[]{:S(2)}) async-start(), calls=%async_computation.4 | async-start | bytes 524288 | tf_op jit(solution)/shard_map/psum | solution.py:36
  201.8 89.5 %all-reduce.32.cloned.1.call-start = ((), (), s32[]{:S(2)}) async-start(), calls=%async_computation.5 | async-start | bytes 262144 | tf_op jit(solution)/shard_map/psum | solution.py:11
  257.0 90.6 %all-reduce.34.cloned.1.call-start = ((), (), s32[]{:S(2)}) async-start(), calls=%async_computation.6 | async-start | bytes 524288 | tf_op jit(solution)/shard_map/psum | solution.py:36
  294.2 89.7 %all-reduce.36.cloned.1.call-start = ((), (), s32[]{:S(2)}) async-start(), calls=%async_computation.7 | async-start | bytes 262144 | tf_op jit(solution)/shard_map/psum | solution.py:11
  349.5 90.7 %all-reduce.38.cloned.1.call-start = ((), (), s32[]{:S(2)}) async-start(), calls=%async_computation.8 | async-start | bytes 524288 | tf_op jit(solution)/shard_map/psum | solution.py:36
  386.8 89.5 %all-reduce.40.cloned.1.call-start = ((), (), s32[]{:S(2)}) async-start(), calls=%async_computation.9 | async-start | bytes 262144 | tf_op jit(solution)/shard_map/psum | solution.py:11
  442.0 90.5 %all-reduce.42.cloned.1.call-start = ((), (), s32[]{:S(2)}) async-start(), calls=%async_computation.10 | async-start | bytes 524288 | tf_op jit(solution)/shard_map/psum | solution.py:36
  479.2 89.5 %all-reduce.44.cloned.1.call-start = ((), (), s32[]{:S(2)}) async-start(), calls=%async_computation.11 | async-start | bytes 262144 | tf_op jit(solution)/shard_map/psum | solution.py:11
  534.4 90.7 %all-reduce.46.cloned.1.call-start = ((), (), s32[]{:S(2)}) async-start(), calls=%async_computation.12 | async-start | bytes 524288 | tf_op jit(solution)/shard_map/psum | solution.py:36
  568.7 139.7 %copy-start.8 = (f32[1,128,256]{2,1,0:T(8,128)S(1)}, f32[1,128,256]{2,1,0:T(8,128)}, u32[]{:S(2)}) copy-start(f32[1,128,256]{2,1,0:T(8,128)} %all-reduce.44.cloned.1.call-done) | copy-start | bytes 393220
  571.7 183.9 %copy-start.7 = (f32[1,128,256]{2,1,0:T(8,128)S(1)}, f32[1,128,256]{2,1,0:T(8,128)}, u32[]{:S(2)}) copy-start(f32[1,128,256]{2,1,0:T(8,128)} %all-reduce.40.cloned.1.call-done) | copy-start | bytes 393220
  571.8 89.5 %all-reduce.48.cloned.1.call-start = ((), (), s32[]{:S(2)}) async-start(), calls=%async_computation.13 | async-start | bytes 262144 | tf_op jit(solution)/shard_map/psum | solution.py:11
  627.0 81.5 %all-reduce.50.cloned.1.call-start = ((), (), s32[]{:S(2)}) async-start(), calls=%async_computation.14 | async-start | bytes 262144 | tf_op jit(solution)/shard_map/psum | solution.py:67
  675.0 128.0 %copy-start.6 = (f32[1,128,256]{2,1,0:T(8,128)S(1)}, f32[1,128,256]{2,1,0:T(8,128)}, u32[]{:S(2)}) copy-start(f32[1,128,256]{2,1,0:T(8,128)} %all-reduce.36.cloned.1.call-done) | copy-start | bytes 393220
  675.0 80.6 %all-reduce.52.cloned.1.call-start = ((), (), s32[]{:S(2)}) async-start(), calls=%async_computation.15 | async-start | bytes 262144 | tf_op jit(solution)/shard_map/psum | solution.py:67
  722.2 80.7 %all-reduce.54.cloned.1.call-start = ((), (), s32[]{:S(2)}) async-start(), calls=%async_computation.16 | async-start | bytes 262144 | tf_op jit(solution)/shard_map/psum | solution.py:67
  769.5 80.7 %all-reduce.56.cloned.1.call-start = ((), (), s32[]{:S(2)}) async-start(), calls=%async_computation.17 | async-start | bytes 262144 | tf_op jit(solution)/shard_map/psum | solution.py:67
  816.9 81.1 %all-reduce.58.cloned.1.call-start = ((), (), s32[]{:S(2)}) async-start(), calls=%async_computation.18 | async-start | bytes 262144 | tf_op jit(solution)/shard_map/psum | solution.py:67
  864.5 80.9 %all-reduce.60.cloned.1.call-start = ((), (), s32[]{:S(2)}) async-start(), calls=%async_computation.19 | async-start | bytes 262144 | tf_op jit(solution)/shard_map/psum | solution.py:67
  912.0 81.0 %all-reduce.62.cloned.1.call-start = ((), (), s32[]{:S(2)}) async-start(), calls=%async_computation.20 | async-start | bytes 262144 | tf_op jit(solution)/shard_map/psum | solution.py:67
  (6 other events, 375.1 us)
Sparse Core Ops, SparseCore 0:
  14.1 56.1 all-reduce.21
  72.7 33.8 all-reduce.23
  109.6 53.1 all-reduce.25
  165.1 33.8 all-reduce.27
  201.9 53.1 all-reduce.29
  257.4 33.8 all-reduce.31
  294.4 53.1 all-reduce.33
  350.0 33.8 all-reduce.35
  387.0 53.1 all-reduce.37
  442.4 33.8 all-reduce.39
  479.4 53.1 all-reduce.41
  534.8 33.8 all-reduce.43
  571.9 53.1 all-reduce.45
  627.4 33.8 all-reduce.47
  675.1 33.2 all-reduce.49
  722.4 33.1 all-reduce.51
  769.6 33.2 all-reduce.53
  817.0 33.1 all-reduce.55
  864.6 33.2 all-reduce.57
  912.2 33.1 all-reduce.59
  959.7 33.2 all-reduce.61
where the time goes:
time: 1000 us
  waiting for transfers between devices  850 us (85%)
  blocking collectives  69.6 us (7%)
  matrix products  49.9 us (5%)
  between operations  14.3 us (1%)
    psum x7, waiting for transfers between devices, per_device(): row_total = lax.psum(partial_sum, 'col')  376 us
    psum x7, waiting for transfers between devices, spread(): return lax.psum(kept, axis)  240 us
    psum x7, waiting for transfers between devices, per_device(): resid = resid - lax.psum(partial_sum, 'row')  234 us
    all_gather x7, blocking collectives, per_device(): pieces = lax.all_gather(low_solved[None], 'col', axis=0, tiled=True)  69.6 us
  transfers between devices with their start and end apart: 21, of which 21 were waited for; matrix products, arithmetic and copies ran while one was open for 0% of the time, Pallas kernels for 0%

commit v1 on v0

--- a/solution.py
+++ b/solution.py
@@ -1,6 +1,10 @@
+import functools
+
 import jax
 import jax.numpy as jnp
 from jax import lax
+from jax.experimental import pallas as pl
+from jax.experimental.pallas import tpu as pltpu
 from jax.sharding import PartitionSpec as P
 
 LEVELS = 8
@@ -78,6 +82,372 @@
     return solution[:, None]
 
 
+MESH = pl.DeviceIdType.MESH
+NT = (((1,), (1,)), ((), ()))
+NN = (((1,), (0,)), ((), ()))
+HIGHEST = lax.Precision.HIGHEST
+
+
+def dot(a, b, dims, precision=None):
+    return lax.dot_general(
+        a, b, dims, precision=precision, preferred_element_type=jnp.float32
+    )
+
+
+def kernel(
+    nz, nc, blk, scen, panel, loads, inverse, out,
+    full, rhs, diag, yval, ylow, xlow, xout, part, sums, landed,
+    own_sem, sib_sem_s, sib_sem_r, chip_sem_s, chip_sem_r,
+    load_own, load_s, load_r, diag_own, diag_s, diag_r, diag_sib_s, diag_sib_r,
+    y_s, y_r, p_s, p_r, out_s, out_r,
+):
+    groups = nc // nz
+    chips = nc // 2
+    span = groups * blk
+    width = scen // nc
+    z = lax.axis_index("row")
+    c = lax.axis_index("col")
+    chip = c // 2
+    core = c % 2
+    sibling = chip * 2 + 1 - core
+    owner = c % nz == z
+    relays = core == z % 2
+    mine = c // nz
+
+    def remote(src, dst, s, r, to):
+        return pltpu.make_async_remote_copy(
+            src_ref=src, dst_ref=dst, send_sem=s, recv_sem=r, device_id=to, device_id_type=MESH
+        )
+
+    barrier = pltpu.get_barrier_semaphore()
+    for step in range(1, nz * nc):
+        other = (z * nc + c + step) % (nz * nc)
+        pl.semaphore_signal(
+            barrier, inc=1, device_id=(other // nc, other % nc), device_id_type=MESH
+        )
+    pl.semaphore_wait(barrier, nz * nc - 1)
+
+    def chunk(ref, level):
+        return ref.at[pl.ds(level * span, span), pl.ds(0, level * blk)]
+
+    def slot(col, level):
+        return full.at[col, pl.ds(level * span, span), pl.ds(0, level * blk)]
+
+    def load_copy(step):
+        to = (c + step) % nc
+        return remote(
+            loads.at[:, pl.ds(to * width, width), :], rhs.at[mine],
+            load_s.at[step], load_r.at[mine], (z, to),
+        )
+
+    def load_self():
+        return pltpu.make_async_copy(
+            loads.at[:, pl.ds(c * width, width), :], rhs.at[mine], load_own
+        )
+
+    def diag_copy(level, step):
+        to = ((chip + step) % chips) * 2 + core
+        return remote(
+            inverse.at[level], diag.at[mine, level],
+            diag_s.at[level, step], diag_r.at[level, mine], (z, to),
+        )
+
+    def diag_self(level):
+        return pltpu.make_async_copy(
+            inverse.at[level], diag.at[mine, level], diag_own.at[level]
+        )
+
+    def diag_sib(level, g):
+        return remote(
+            diag.at[g, level], diag.at[g, level],
+            diag_sib_s.at[level, g], diag_sib_r.at[level, g], (z, sibling),
+        )
+
+    def chip_copy(level, step):
+        to = ((chip + step) % chips) * 2 + core
+        return remote(
+            chunk(panel, level), slot(c, level),
+            chip_sem_s.at[level, step], chip_sem_r.at[level, step], (z, to),
+        )
+
+    def own_copy(level):
+        return pltpu.make_async_copy(chunk(panel, level), slot(c, level), own_sem.at[level])
+
+    def sib_copy(level, step):
+        if step == 0:
+            src, col = chunk(panel, level), c
+        else:
+            col = ((chip + chips - step) % chips) * 2 + core
+            src = slot(col, level)
+        return remote(
+            src, slot(col, level),
+            sib_sem_s.at[level, step], sib_sem_r.at[level, step], (z, sibling),
+        )
+
+    @pl.when(owner)
+    def _():
+        load_self().start()
+        for step in range(1, nc):
+            load_copy(step).start()
+
+    for level in range(LEVELS):
+        @pl.when(owner)
+        def _():
+            diag_self(level).start()
+            for step in range(1, chips):
+                diag_copy(level, step).start()
+
+        if level > 0:
+            for step in range(1, chips):
+                chip_copy(level, step).start()
+            own_copy(level).start()
+            sib_copy(level, 0).start()
+
+    def relay(level):
+        @pl.when(relays)
+        def _():
+            for g in range(groups):
+                @pl.when(c == z + nz * g)
+                def _():
+                    diag_self(level).wait()
+
+                @pl.when(c != z + nz * g)
+                def _():
+                    remote(
+                        diag.at[g, level], diag.at[g, level], diag_s.at[level, 0],
+                        diag_r.at[level, g], (z, sibling),
+                    ).wait_recv()
+
+                diag_sib(level, g).start()
+
+        if level > 0:
+            for step in range(1, chips):
+                chip_copy(level, step).wait_recv()
+                sib_copy(level, step).start()
+
+    def arrived(level):
+        @pl.when(jnp.logical_not(relays))
+        def _():
+            for g in range(groups):
+                diag_sib(level, g).wait_recv()
+
+        if level > 0:
+            own_copy(level).wait()
+            for step in range(chips):
+                sib_copy(level, step).wait_recv()
+
+    def y_copy(level, step):
+        here = ylow.at[z, :, :, pl.ds(level * blk, blk)]
+        return remote(
+            here, here, y_s.at[level, step], y_r.at[level, step], ((z + step) % nz, c)
+        )
+
+    def column(col, low, high):
+        return ylow[col % nz, col // nz, :, low * blk : high * blk]
+
+    relay(0)
+    for g in range(groups):
+        @pl.when(c != z + nz * g)
+        def _():
+            remote(
+                rhs.at[g], rhs.at[g], load_s.at[0], load_r.at[g], (z, sibling)
+            ).wait_recv()
+
+    @pl.when(owner)
+    def _():
+        load_self().wait()
+
+    for level in range(LEVELS):
+        arrived(level)
+        if level > 0:
+            total = jnp.zeros((width, span), jnp.float32)
+            rows = pl.ds(level * span, span)
+            if level > 1:
+                def far(col, acc):
+                    known = ylow[col % nz, col // nz, :, pl.ds(0, (level - 1) * blk)]
+                    return acc + dot(known, full[col, rows, pl.ds(0, (level - 1) * blk)], NT)
+
+                total = lax.fori_loop(0, nc, far, total)
+            for step in range(1, nz):
+                y_copy(level - 1, step).wait_recv()
+            for col in range(nc):
+                near = full[col, rows, pl.ds((level - 1) * blk, blk)]
+                total = total + dot(column(col, level - 1, level), near, NT)
+        for g in range(groups):
+            resid = rhs[g, level]
+            if level > 0:
+                resid = resid - total[:, g * blk : (g + 1) * blk]
+            solved = dot(resid, diag[g, level], NT, HIGHEST)
+            yval[g, level] = solved
+            if level < LEVELS - 1:
+                ylow[z, g, :, level * blk : (level + 1) * blk] = solved.astype(jnp.bfloat16)
+        if level < LEVELS - 1:
+            for step in range(1, nz):
+                y_copy(level, step).start()
+            relay(level + 1)
+
+    def part_copy(level, step):
+        to = (z + step) % nz
+        return remote(
+            part.at[level, to], sums.at[level, z],
+            p_s.at[level, step], p_r.at[level, step], (to, c),
+        )
+
+    def out_copy(level, step, g):
+        return remote(
+            xout.at[level, g], landed.at[level, c],
+            out_s.at[level, step, g], out_r.at[level], ((z + step) % nz, z + nz * g),
+        )
+
+    def out_self(level, g):
+        return pltpu.make_async_copy(xout.at[level, g], landed.at[level, c], out_r.at[level])
+
+    for level in reversed(range(LEVELS)):
+        if level < LEVELS - 1:
+            lanes = pl.ds(level * blk, blk)
+            first = (level + 1) * span
+            second = first + span
+            late = LEVELS * span
+            near_x = xlow[:, first:second]
+            for col in range(nc):
+                value = dot(near_x, full[col, first:second, lanes], NN)
+                if level < LEVELS - 2:
+                    value = value + farsum[col]
+                part[level, col % nz, col // nz] = value.astype(jnp.bfloat16)
+            for step in range(1, nz):
+                part_copy(level, step).start()
+        if 0 < level:
+            ahead = pl.ds((level - 1) * blk, blk)
+        if level < LEVELS - 1:
+            for step in range(1, nz):
+                part_copy(level, step).wait_recv()
+        for g in range(groups):
+            resid = yval[g, level]
+            if level < LEVELS - 1:
+                for step in range(nz):
+                    if step == 0:
+                        piece = part[level, z, g]
+                    else:
+                        piece = sums[level, (z + nz - step) % nz, g]
+                    resid = resid - piece.astype(jnp.float32)
+            solved = dot(resid, diag[g, level], NN, HIGHEST)
+            low = solved.astype(jnp.bfloat16)
+            xout[level, g] = low
+            if level > 0:
+                at = level * span + g * blk
+                xlow[:, at : at + blk] = low
+        for g in range(groups):
+            @pl.when(c == z + nz * g)
+            def _():
+                out_self(level, g).start()
+
+            @pl.when(c != z + nz * g)
+            def _():
+                out_copy(level, 0, g).start()
+
+            for step in range(1, nz):
+                out_copy(level, step, g).start()
+        if 0 < level < LEVELS - 1:
+            low_row = (level + 1) * span
+            known = xlow[:, low_row:]
+            farsum = [dot(known, full[col, low_row:, ahead], NN) for col in range(nc)]
+
+    for level in range(LEVELS):
+        pltpu.make_async_copy(landed.at[level], landed.at[level], out_r.at[level]).wait()
+    out[...] = landed[...]
+
+    @pl.when(owner)
+    def _():
+        for step in range(1, nc):
+            load_copy(step).wait_send()
+
+    for level in range(LEVELS):
+        @pl.when(owner)
+        def _():
+            for step in range(1, chips):
+                diag_copy(level, step).wait_send()
+
+        @pl.when(relays)
+        def _():
+            for g in range(groups):
+                diag_sib(level, g).wait_send()
+
+        if level > 0:
+            for step in range(1, chips):
+                chip_copy(level, step).wait_send()
+            for step in range(chips):
+                sib_copy(level, step).wait_send()
+        if level < LEVELS - 1:
+            for step in range(1, nz):
+                y_copy(level, step).wait_send()
+                part_copy(level, step).wait_send()
+        for g in range(groups):
+            @pl.when(c != z + nz * g)
+            def _():
+                out_copy(level, 0, g).wait_send()
+
+            for step in range(1, nz):
+                out_copy(level, step, g).wait_send()
+
+
+def replicated_plan(factor, pattern, loads, block_inverse):
+    nz, nc = lax.axis_size("row"), lax.axis_size("col")
+    rows, cols, blk = factor.shape[0], factor.shape[2], factor.shape[4]
+    scen = loads.shape[3]
+    groups, chips, width = nc // nz, nc // 2, scen // nc
+    masked = factor[:, 0, :, 0] * pattern[:, 0, :, 0].astype(jnp.bfloat16)[:, :, None, None]
+    panel = jnp.swapaxes(masked, 1, 2).reshape(rows * blk, cols * blk)
+    turned = jnp.swapaxes(loads[:, 0], 1, 2)
+    low, f32 = jnp.bfloat16, jnp.float32
+    dma = pltpu.SemaphoreType.DMA
+    vmem = pl.BlockSpec(memory_space=pltpu.VMEM)
+    result = pl.pallas_call(
+        functools.partial(kernel, nz, nc, blk, scen),
+        out_shape=jax.ShapeDtypeStruct((LEVELS, nc, width, blk), low),
+        in_specs=[pl.BlockSpec(memory_space=pl.ANY), vmem, vmem],
+        out_specs=vmem,
+        scratch_shapes=[
+            pltpu.VMEM((nc, rows * blk, cols * blk), low),
+            pltpu.VMEM((groups, LEVELS, width, blk), f32),
+            pltpu.VMEM((groups, LEVELS, blk, blk), f32),
+            pltpu.VMEM((groups, LEVELS, width, blk), f32),
+            pltpu.VMEM((nz, groups, width, LEVELS * blk), low),
+            pltpu.VMEM((width, rows * blk), low),
+            pltpu.VMEM((LEVELS, groups, width, blk), low),
+            pltpu.VMEM((LEVELS, nz, groups, width, blk), low),
+            pltpu.VMEM((LEVELS, nz, groups, width, blk), low),
+            pltpu.VMEM((LEVELS, nc, width, blk), low),
+            dma((LEVELS,)),
+            dma((LEVELS, chips)), dma((LEVELS, chips)),
+            dma((LEVELS, chips)), dma((LEVELS, chips)),
+            dma, dma((nc,)), dma((groups,)),
+            dma((LEVELS,)), dma((LEVELS, chips)), dma((LEVELS, groups)),
+            dma((LEVELS, groups)), dma((LEVELS, groups)),
+            dma((LEVELS, nz)), dma((LEVELS, nz)),
+            dma((LEVELS, nz)), dma((LEVELS, nz)),
+            dma((LEVELS, nz, groups)), dma((LEVELS,)),
+        ],
+        compiler_params=pltpu.CompilerParams(
+            collective_id=0, has_side_effects=True, vmem_limit_bytes=52 * 2**20
+        ),
+    )(panel, turned, block_inverse[:, 0])
+    result = result.reshape(LEVELS, scen, blk).astype(f32)
+    return jnp.swapaxes(result, 1, 2)[:, None]
+
+
+def pick_plan(mesh):
+    def plan(factor, pattern, loads, block_inverse):
+        nz, nc = mesh.shape["row"], mesh.shape["col"]
+        scen = loads.shape[3]
+        small = nc * factor.size * 2 <= 32 * 2**20
+        even = nc % nz == 0 and nc % 2 == 0 and nz % 2 == 0 and scen % (16 * nc) == 0
+        if small and even and loads.shape[0] == LEVELS:
+            return replicated_plan(factor, pattern, loads, block_inverse)
+        return per_device(factor, pattern, loads, block_inverse)
+
+    return plan
+
+
 def solution(mesh):
     in_specs = (
         P(None, "row", None, "col", None, None),
@@ -87,5 +457,5 @@
     )
     out_specs = P(None, "col", None, None)
     return jax.shard_map(
-        per_device, mesh=mesh, in_specs=in_specs, out_specs=out_specs, check_vma=False
+        pick_plan(mesh), mesh=mesh, in_specs=in_specs, out_specs=out_specs, check_vma=False
     )

time: 1000 us -> 166 us (0.17)
  waiting for transfers between devices: 850 us -> 0 us
  Pallas kernels: 0 us -> 153 us
  blocking collectives: 69.6 us -> 0 us
  matrix products: 49.9 us -> 0 us
  between operations: 14.3 us -> 0.05 us
    psum x21 -> x0, waiting for transfers between devices: 850 us -> none  [the longest x7 376 us: per_device(): row_total = lax.psum(partial_sum, 'col')]
    pallas_call x0 -> x1, Pallas kernels: none -> 153 us  [replicated_plan(): pl.pallas_call(functools.partial(kernel, nz, nc, blk, scen), out_shape=ja...]
    all_gather x7 -> x0, blocking collectives: 69.6 us -> none  [per_device(): pieces = lax.all_gather(low_solved[None], 'col', axis=0, tiled=True)]
    dot_general x30 -> x0, matrix products: 49.9 us -> none  [the longest x7 13.1 us: per_device(): jnp.einsum('abpq,aps->bqs', panel, after, preferred_element_type=jnp.floa...]
  transfers between devices with their start and end apart: 21 -> 0, of which waited for: 21 -> 0; matrix products, arithmetic and copies ran while one was open for 0% -> 0% of each run, Pallas kernels for 0% -> 0%
where the time goes in v1:
time: 166 us
  Pallas kernels  153 us (92%)
  local copies, waits for them, and re-layouts  9.31 us (6%)
  other arithmetic  3.32 us (2%)
    pallas_call x1, Pallas kernels, replicated_plan(): pl.pallas_call(functools.partial(kernel, nz, nc, blk, scen), out_shape=ja...  153 us
    unnamed x6, local copies, waits for them, and re-layouts  4.38 us
    transpose x1, local copies, waits for them, and re-layouts, replicated_plan(): panel = jnp.swapaxes(masked, 1, 2).reshape(rows * blk, cols * blk)  3.54 us

profile of v1, /device:TPU:0, one launch (start us, length us, event | category | flops | bytes accessed | tf_op | source)
XLA Modules:
  0.0 165.5 jit_solution(4120936193207855762)
XLA Ops:
  0.0 0.7 convert_bitcast_fusion
  0.7 0.1 copy.6
  0.8 2.5 %fusion = bf16[16,128,8,128]{3,1,2,0:T(8,128)(2,1)S(1)} fusion(bf16[16,1,8,1,128,128]{5,4,3,2,1,0:T(8,128)(2,1)} %param.4, bf16[16,8]{1,0:T(8,128)(2,1)S(1)} %copy.6), kind=kLoop, calls=%fused_computation.2 | loop fusion | flops 2097152 | bytes 8388864 | tf_op jit(solution)/shard_map/transpose | solution.py:399
  3.3 3.5 %copy.7 = bf16[16,128,8,128]{3,2,1,0:T(8,128)(2,1)S(1)} copy(bf16[16,128,8,128]{3,1,2,0:T(8,128)(2,1)S(1)} %fusion) | data formatting | bytes 8388608 | tf_op jit(solution)/shard_map/transpose | solution.py:399
  6.9 0.0 copy-start.1
  6.9 0.0 copy-start
  6.9 3.1 %copy.12 = bf16[256,8,8,128]{3,1,2,0:T(8,128)(2,1)} copy(bf16[256,8,8,128]{3,2,1,0:T(8,128)(2,1)S(1)} %bitcast.26) | data formatting | bytes 8388608
  9.9 0.0 copy-done.1
  9.9 1.3 copy.8
  11.2 0.0 copy-done
  11.3 152.9 %shard_map.46 = bf16[8,8,32,128]{3,2,1,0:T(8,128)(2,1)S(1)} custom-call(bf16[2048,1024]{1,0:T(8,128)(2,1)} %bitcast.25, f32[8,256,128]{2,1,0:T(8,128)} %bitcast.27, f32[8,128,128]{2,1,0:T(8,128)S(1)} %bitcast.24), custom_call_target="tpu_custom_call" | custom-call | tf_op jit(solution)/shard_map/pallas_call | solution.py:404
  164.1 0.1 bitcast_convert_fusion
  164.2 1.3 copy.9
Async XLA Ops:
  6.9 3.1 %copy-start.1 = (f32[8,1,128,256]{3,2,1,0:T(8,128)S(1)}, f32[8,1,128,256]{3,2,1,0:T(8,128)}, u32[]{:S(2)}) copy-start(f32[8,1,128,256]{3,2,1,0:T(8,128)} %param.6) | copy-start | bytes 3145732
  6.9 4.4 %copy-start = (f32[8,1,128,128]{3,2,1,0:T(8,128)S(1)}, f32[8,1,128,128]{3,2,1,0:T(8,128)}, u32[]{:S(2)}) copy-start(f32[8,1,128,128]{3,2,1,0:T(8,128)} %param.7) | copy-start | bytes 1572868

commit v2 on v1

v2 whole, which is shorter than its diff:
```python
import functools

import jax
import jax.numpy as jnp
from jax import lax
from jax.experimental import pallas as pl
from jax.experimental.pallas import tpu as pltpu
from jax.sharding import PartitionSpec as P

LEVELS = 8


def spread(value, axis, source):
    kept = jnp.where(lax.axis_index(axis) == source, value, 0).astype(value.dtype)
    return lax.psum(kept, axis)


def per_device(factor, pattern, loads, block_inverse):
    row_count = lax.axis_size("row")
    col_count = lax.axis_size("col")
    groups = col_count // row_count
    my_row = lax.axis_index("row")
    my_col = lax.axis_index("col")
    masked = factor[:, 0, :, 0] * pattern[:, 0, :, 0].astype(jnp.bfloat16)[:, :, None, None]
    per_row = factor.shape[0] // LEVELS
    per_col = factor.shape[2] // LEVELS
    rhs_local = loads[:, 0]
    inverse_local = block_inverse[:, 0]
    forward_vals = []
    forward_low = []
    for level_id in range(LEVELS):
        rhs_level = rhs_local[level_id * per_col : (level_id + 1) * per_col]
        inverse_level = inverse_local[level_id * per_col : (level_id + 1) * per_col]
        if level_id > 0:
            panel = masked[level_id * per_row : (level_id + 1) * per_row, : level_id * per_col]
            earlier = jnp.concatenate(forward_low, axis=0)
            partial_sum = jnp.einsum(
                "abpq,bqs->aps", panel, earlier, preferred_element_type=jnp.float32
            )
            row_total = lax.psum(partial_sum, "col")
            row_total = row_total.reshape((per_col, groups) + row_total.shape[1:])
            own_total = lax.dynamic_index_in_dim(
                row_total, my_col // row_count, axis=1, keepdims=False
            )
            solved = jnp.einsum(
                "mpq,mqs->mps",
                inverse_level,
                rhs_level - own_total,
                precision=lax.Precision.HIGHEST,
            )
            solved = spread(solved, "row", my_col % row_count)
        else:
            solved = jnp.einsum(
                "mpq,mqs->mps", inverse_level, rhs_level, precision=lax.Precision.HIGHEST
            )
        forward_vals.append(solved)
        forward_low.append(solved.astype(jnp.bfloat16))
    solution_parts = [None] * LEVELS
    later = []
    for level_id in reversed(range(LEVELS)):
        inverse_level = inverse_local[level_id * per_col : (level_id + 1) * per_col]
        resid = forward_vals[level_id]
        if level_id < LEVELS - 1:
            panel = masked[
                (level_id + 1) * per_row :, level_id * per_col : (level_id + 1) * per_col
            ]
            after = jnp.concatenate(later, axis=0)
            partial_sum = jnp.einsum(
                "abpq,aps->bqs", panel, after, preferred_element_type=jnp.float32
            )
            resid = resid - lax.psum(partial_sum, "row")
        solved = jnp.einsum("mqp,mqs->mps", inverse_level, resid, precision=lax.Precision.HIGHEST)
        solution_parts[level_id] = solved
        if level_id > 0:
            low_solved = solved.astype(jnp.bfloat16)
            pieces = lax.all_gather(low_solved[None], "col", axis=0, tiled=True)
            pieces = pieces.reshape((groups, row_count) + low_solved.shape)
            picked = lax.dynamic_index_in_dim(pieces, my_row, axis=1, keepdims=False)
            arranged = jnp.swapaxes(picked, 0, 1).reshape((per_row,) + low_solved.shape[1:])
            later = [arranged] + later
    solution = jnp.concatenate(solution_parts, axis=0)
    return solution[:, None]


MESH = pl.DeviceIdType.MESH
NT = (((1,), (1,)), ((), ()))
NN = (((1,), (0,)), ((), ()))
HIGHEST = lax.Precision.HIGHEST


def dot(a, b, dims, precision=None):
    return lax.dot_general(
        a, b, dims, precision=precision, preferred_element_type=jnp.float32
    )


def kernel(
    nz, nc, blk, scen, factor, pattern, loads, inverse, out,
    near, own, rhs, diag, yval, ylow, yfull, fpart, fsum, xlow, xfull,
    part, sums, bpart, bsum, landed,
    sib_s, sib_r, chip_s, chip_r,
    load_own, load_s, load_r, diag_own, diag_s, diag_r, diag_sib_s, diag_sib_r,
    y_s, y_r, yf_s, yf_r, f_s, f_r, p_s, p_r, xf_s, xf_r, b_s, b_r, out_s, out_r,
):
    groups = nc // nz
    chips = nc // 2
    width = scen // nc
    last = LEVELS - 1
    z = lax.axis_index("row")
    c = lax.axis_index("col")
    chip = c // 2
    core = c % 2
    sibling = chip * 2 + 1 - core
    owner = c % nz == z
    relays = core == z % 2
    mine = c // nz

    def remote(src, dst, s, r, to):
        return pltpu.make_async_remote_copy(
            src_ref=src, dst_ref=dst, send_sem=s, recv_sem=r, device_id=to, device_id_type=MESH
        )

    def share(col):
        return pl.ds(pl.multiple_of(col * width, width), width)

    def masked(row, col):
        return factor[row, col] * pattern[row, col].astype(jnp.float32).astype(jnp.bfloat16)

    for level in range(1, LEVELS):
        for g in range(groups):
            near[c, level, g * blk : (g + 1) * blk] = masked(level * groups + g, level - 1)

    barrier = pltpu.get_barrier_semaphore()
    for step in range(1, nz * nc):
        other = (z * nc + c + step) % (nz * nc)
        pl.semaphore_signal(
            barrier, inc=1, device_id=(other // nc, other % nc), device_id_type=MESH
        )
    pl.semaphore_wait(barrier, nz * nc - 1)

    def load_copy(step):
        to = (c + step) % nc
        return remote(
            loads.at[:, share(to), :], rhs.at[mine],
            load_s.at[step], load_r.at[mine], (z, to),
        )

    def load_self():
        return pltpu.make_async_copy(loads.at[:, share(c), :], rhs.at[mine], load_own)

    def diag_copy(level, step):
        to = ((chip + step) % chips) * 2 + core
        return remote(
            inverse.at[level], diag.at[mine, level],
            diag_s.at[level, step], diag_r.at[level, mine], (z, to),
        )

    def diag_self(level):
        return pltpu.make_async_copy(
            inverse.at[level], diag.at[mine, level], diag_own.at[level]
        )

    def diag_sib(level, g):
        return remote(
            diag.at[g, level], diag.at[g, level],
            diag_sib_s.at[level, g], diag_sib_r.at[level, g], (z, sibling),
        )

    def chip_copy(level, step):
        to = ((chip + step) % chips) * 2 + core
        here = near.at[c, level]
        return remote(here, here, chip_s.at[level, step], chip_r.at[level, step], (z, to))

    def sib_copy(level, step):
        here = near.at[((chip + chips - step) % chips) * 2 + core, level]
        return remote(here, here, sib_s.at[level, step], sib_r.at[level, step], (z, sibling))

    @pl.when(owner)
    def _():
        load_self().start()
        for step in range(1, nc):
            load_copy(step).start()

    for level in range(LEVELS):
        @pl.when(owner)
        def _():
            diag_self(level).start()
            for step in range(1, chips):
                diag_copy(level, step).start()

        if level > 0:
            for step in range(1, chips):
                chip_copy(level, step).start()
            sib_copy(level, 0).start()

    for level in range(2, LEVELS):
        for g in range(groups):
            for col in range(level - 1):
                own[level * groups + g, col] = masked(level * groups + g, col)

    def relay(level):
        @pl.when(relays)
        def _():
            for g in range(groups):
                @pl.when(c == z + nz * g)
                def _():
                    diag_self(level).wait()

                @pl.when(c != z + nz * g)
                def _():
                    remote(
                        diag.at[g, level], diag.at[g, level], diag_s.at[level, 0],
                        diag_r.at[level, g], (z, sibling),
                    ).wait_recv()

                diag_sib(level, g).start()

        if level > 0:
            for step in range(1, chips):
                chip_copy(level, step).wait_recv()
                sib_copy(level, step).start()

    def arrived(level):
        @pl.when(jnp.logical_not(relays))
        def _():
            for g in range(groups):
                diag_sib(level, g).wait_recv()

        if level > 0:
            for step in range(chips):
                sib_copy(level, step).wait_recv()

    def spread_sent(level):
        @pl.when(owner)
        def _():
            for step in range(1, chips):
                diag_copy(level, step).wait_send()

        @pl.when(relays)
        def _():
            for g in range(groups):
                diag_sib(level, g).wait_send()

        if level > 0:
            for step in range(1, chips):
                chip_copy(level, step).wait_send()
            for step in range(chips):
                sib_copy(level, step).wait_send()

    def y_copy(level, step):
        here = ylow.at[level, z]
        return remote(
            here, here, y_s.at[level, step], y_r.at[level, step], ((z + step) % nz, c)
        )

    def to_columns(src, dst, s, r, act):
        for g in range(groups):
            for step in range(nz):
                def go():
                    copy = remote(
                        src.at[g], dst, s.at[step, g], r, ((z + step) % nz, z + nz * g)
                    )
                    copy.start() if act else copy.wait_send()

                if step > 0:
                    go()
                else:
                    pl.when(c != z + nz * g)(go)
                    if act:
                        @pl.when(c == z + nz * g)
                        def _():
                            pltpu.make_async_copy(src.at[g], dst, r).start()

    def y_far(level, act):
        to_columns(
            ylow.at[level, z], yfull.at[level, share(c), :], yf_s.at[level], yf_r.at[level], act
        )

    def out_far(level, act):
        to_columns(xlow.at[level], landed.at[level, c], out_s.at[level], out_r.at[level], act)

    def f_far(level, act):
        for step in range(1, nc):
            to = (c + step) % nc
            copy = remote(
                fpart.at[level, :, share(to), :], fsum.at[level, c],
                f_s.at[level, step], f_r.at[level], (z, to),
            )
            copy.start() if act else copy.wait_send()
        if act:
            pltpu.make_async_copy(
                fpart.at[level, :, share(c), :], fsum.at[level, c], f_r.at[level]
            ).start()

    def x_far(level, act):
        here = xfull.at[level, :, share(c), :]
        for step in range(1, nc):
            copy = remote(
                xlow.at[level], here, xf_s.at[level, step], xf_r.at[level], (z, (c + step) % nc)
            )
            copy.start() if act else copy.wait_send()
        if act:
            pltpu.make_async_copy(xlow.at[level], here, xf_r.at[level]).start()

    def b_far(level, act):
        for step in range(nc):
            to = (c + step) % nc
            src, dst = bpart.at[level, share(to), :], bsum.at[level, z, mine]

            def go():
                copy = remote(src, dst, b_s.at[level, step], b_r.at[level], (c % nz, to))
                copy.start() if act else copy.wait_send()

            if step > 0:
                go()
            else:
                pl.when(jnp.logical_not(owner))(go)
                if act:
                    @pl.when(owner)
                    def _():
                        pltpu.make_async_copy(src, dst, b_r.at[level]).start()

    def all_in(ref, sem):
        pltpu.make_async_copy(ref, ref, sem).wait()

    relay(0)
    for g in range(groups):
        @pl.when(c != z + nz * g)
        def _():
            remote(
                rhs.at[g], rhs.at[g], load_s.at[0], load_r.at[g], (z, sibling)
            ).wait_recv()

    @pl.when(owner)
    def _():
        load_self().wait()

    for level in range(LEVELS):
        arrived(level)
        resid = [rhs[g, level] for g in range(groups)]
        if level > 1:
            all_in(fsum.at[level], f_r.at[level])
            for g in range(groups):
                for col in range(nc):
                    resid[g] = resid[g] - fsum[level, col, g].astype(jnp.float32)
        if level > 0:
            for step in range(1, nz):
                y_copy(level - 1, step).wait_recv()
            total = jnp.zeros((width, groups * blk), jnp.float32)
            for col in range(nc):
                total = total + dot(ylow[level - 1, col % nz, col // nz], near[col, level], NT)
            resid = [resid[g] - total[:, g * blk : (g + 1) * blk] for g in range(groups)]
        for g in range(groups):
            solved = dot(resid[g], diag[g, level], NT, HIGHEST)
            yval[g, level] = solved
            if level < last:
                ylow[level, z, g] = solved.astype(jnp.bfloat16)
        if level < last:
            for step in range(1, nz):
                y_copy(level, step).start()
            if level > 0:
                all_in(yfull.at[level - 1], yf_r.at[level - 1])
                for g in range(groups):
                    row = (level + 1) * groups + g
                    value = dot(yfull[0], own[row, 0], NT)
                    for col in range(1, level):
                        value = value + dot(yfull[col], own[row, col], NT)
                    fpart[level + 1, g] = value.astype(jnp.bfloat16)
                f_far(level + 1, True)
            if level < last - 1:
                y_far(level, True)
            relay(level + 1)
            if level > 0:
                for step in range(1, nz):
                    y_copy(level - 1, step).wait_send()
                y_far(level - 1, False)
                spread_sent(level - 1)
            if level > 1:
                f_far(level, False)

    def part_copy(level, step):
        to = (z + step) % nz
        return remote(
            part.at[level, to], sums.at[level, z],
            p_s.at[level, step], p_r.at[level, step], (to, c),
        )

    for level in reversed(range(LEVELS)):
        if level < last:
            above = jnp.concatenate([xlow[level + 1, g] for g in range(groups)], axis=1)
            for col in range(nc):
                value = dot(above, near[col, level + 1], NN)
                part[level, col % nz, col // nz] = value.astype(jnp.bfloat16)
            for step in range(1, nz):
                part_copy(level, step).start()
            if level < last - 1:
                all_in(xfull.at[level + 2], xf_r.at[level + 2])
                value = None
                for up in range(level + 2, LEVELS):
                    for g in range(groups):
                        term = dot(xfull[up, g], own[up * groups + g, level], NN)
                        value = term if value is None else value + term
                bpart[level] = value.astype(jnp.bfloat16)
                b_far(level, True)
            if level > 0:
                x_far(level + 1, True)
            out_far(level + 1, True)
            if level == last - 1:
                for step in range(1, nz):
                    y_copy(last - 1, step).wait_send()
                f_far(last, False)
                spread_sent(last - 1)
                spread_sent(last)

                @pl.when(owner)
                def _():
                    for step in range(1, nc):
                        load_copy(step).wait_send()
            else:
                for step in range(1, nz):
                    part_copy(level + 1, step).wait_send()
                x_far(level + 2, False)
                out_far(level + 2, False)
                all_in(landed.at[level + 2], out_r.at[level + 2])
            if level < last - 2:
                b_far(level + 1, False)
            for step in range(1, nz):
                part_copy(level, step).wait_recv()
            if level < last - 1:
                all_in(bsum.at[level], b_r.at[level])
        for g in range(groups):
            resid = yval[g, level]
            if level < last:
                for step in range(nz):
                    if step == 0:
                        piece = part[level, z, g]
                    else:
                        piece = sums[level, (z + nz - step) % nz, g]
                    resid = resid - piece.astype(jnp.float32)
                    if level < last - 1:
                        resid = resid - bsum[level, step, g].astype(jnp.float32)
            xlow[level, g] = dot(resid, diag[g, level], NN, HIGHEST).astype(jnp.bfloat16)

    out_far(0, True)
    for step in range(1, nz):
        part_copy(0, step).wait_send()
    b_far(0, False)
    out_far(1, False)
    all_in(landed.at[1], out_r.at[1])
    out[1:] = landed[1:]
    out_far(0, False)
    all_in(landed.at[0], out_r.at[0])
    out[0] = landed[0]


def split_plan(factor, pattern, loads, block_inverse):
    nz, nc = lax.axis_size("row"), lax.axis_size("col")
    rows, cols, blk = factor.shape[0], factor.shape[2], factor.shape[4]
    scen = loads.shape[3]
    groups, chips, width = nc // nz, nc // 2, scen // nc
    turned = jnp.swapaxes(loads[:, 0], 1, 2)
    low, f32 = jnp.bfloat16, jnp.float32
    dma = pltpu.SemaphoreType.DMA
    vmem = pl.BlockSpec(memory_space=pltpu.VMEM)
    smem = pl.BlockSpec(memory_space=pltpu.SMEM)
    result = pl.pallas_call(
        functools.partial(kernel, nz, nc, blk, scen),
        out_shape=jax.ShapeDtypeStruct((LEVELS, nc, width, blk), low),
        in_specs=[vmem, smem, vmem, vmem],
        out_specs=vmem,
        scratch_shapes=[
            pltpu.VMEM((nc, LEVELS, groups * blk, blk), low),
            pltpu.VMEM((rows, cols, blk, blk), low),
            pltpu.VMEM((groups, LEVELS, width, blk), f32),
            pltpu.VMEM((groups, LEVELS, blk, blk), f32),
            pltpu.VMEM((groups, LEVELS, width, blk), f32),
            pltpu.VMEM((LEVELS, nz, groups, width, blk), low),
            pltpu.VMEM((LEVELS, scen, blk), low),
            pltpu.VMEM((LEVELS, groups, scen, blk), low),
            pltpu.VMEM((LEVELS, nc, groups, width, blk), low),
            pltpu.VMEM((LEVELS, groups, width, blk), low),
            pltpu.VMEM((LEVELS, groups, scen, blk), low),
            pltpu.VMEM((LEVELS, nz, groups, width, blk), low),
            pltpu.VMEM((LEVELS, nz, groups, width, blk), low),
            pltpu.VMEM((LEVELS, scen, blk), low),
            pltpu.VMEM((LEVELS, nz, groups, width, blk), low),
            pltpu.VMEM((LEVELS, nc, width, blk), low),
            dma((LEVELS, chips)), dma((LEVELS, chips)),
            dma((LEVELS, chips)), dma((LEVELS, chips)),
            dma, dma((nc,)), dma((groups,)),
            dma((LEVELS,)), dma((LEVELS, chips)), dma((LEVELS, groups)),
            dma((LEVELS, groups)), dma((LEVELS, groups)),
            dma((LEVELS, nz)), dma((LEVELS, nz)),
            dma((LEVELS, nz, groups)), dma((LEVELS,)),
            dma((LEVELS, nc)), dma((LEVELS,)),
            dma((LEVELS, nz)), dma((LEVELS, nz)),
            dma((LEVELS, nc)), dma((LEVELS,)),
            dma((LEVELS, nc)), dma((LEVELS,)),
            dma((LEVELS, nz, groups)), dma((LEVELS,)),
        ],
        compiler_params=pltpu.CompilerParams(
            collective_id=0, has_side_effects=True, vmem_limit_bytes=52 * 2**20
        ),
    )(factor[:, 0, :, 0], pattern[:, 0, :, 0], turned, block_inverse[:, 0])
    result = result.reshape(LEVELS, scen, blk).astype(f32)
    return jnp.swapaxes(result, 1, 2)[:, None]


def pick_plan(mesh):
    def plan(factor, pattern, loads, block_inverse):
        nz, nc = mesh.shape["row"], mesh.shape["col"]
        scen = loads.shape[3]
        small = nc * factor.size * 2 <= 32 * 2**20
        single = factor.shape[2] == LEVELS and factor.shape[0] == LEVELS * (nc // nz)
        even = nc % nz == 0 and nc % 2 == 0 and nz % 2 == 0 and scen % (16 * nc) == 0
        if small and even and single and loads.shape[0] == LEVELS:
            return split_plan(factor, pattern, loads, block_inverse)
        return per_device(factor, pattern, loads, block_inverse)

    return plan


def solution(mesh):
    in_specs = (
        P(None, "row", None, "col", None, None),
        P(None, "row", None, "col"),
        P(None, "col", None, None),
        P(None, "col", None, None),
    )
    out_specs = P(None, "col", None, None)
    return jax.shard_map(
        pick_plan(mesh), mesh=mesh, in_specs=in_specs, out_specs=out_specs, check_vma=False
    )
```

time: 166 us -> 143 us (0.86)
  Pallas kernels: 153 us -> 137 us
  local copies, waits for them, and re-layouts: 9.31 us -> 5.63 us
  other arithmetic: 3.32 us -> 0.1 us
    pallas_call x1, Pallas kernels: 153 us -> 137 us  [split_plan(): pl.pallas_call(functools.partial(kernel, nz, nc, blk, scen), out_shape=ja...]
    transpose x1 -> x0, local copies, waits for them, and re-layouts: 3.54 us -> none  [replicated_plan(): panel = jnp.swapaxes(masked, 1, 2).reshape(rows * blk, cols * blk)]
    transpose x1 -> x0, other arithmetic: 2.53 us -> none  [replicated_plan(): panel = jnp.swapaxes(masked, 1, 2).reshape(rows * blk, cols * blk)]
    unnamed x6 -> x3, local copies, waits for them, and re-layouts: 4.38 us -> 3.57 us
where the time goes in v2:
time: 143 us
  Pallas kernels  137 us (96%)
  local copies, waits for them, and re-layouts  5.63 us (4%)
    pallas_call x1, Pallas kernels, split_plan(): pl.pallas_call(functools.partial(kernel, nz, nc, blk, scen), out_shape=ja...  137 us
    unnamed x3, local copies, waits for them, and re-layouts  3.57 us

profile of v2, /device:TPU:0, one launch (start us, length us, event | category | flops | bytes accessed | tf_op | source)
XLA Modules:
  0.0 142.7 jit_solution(16804148121251318080)
XLA Ops:
  0.0 0.8 copy.6.pattern
  0.8 2.5 %copy.5 = f32[8,1,128,256]{2,3,0,1:T(8,128)} copy(f32[8,1,128,256]{3,2,1,0:T(8,128)} %param.6) | data formatting | bytes 2097152 | tf_op args[2]
  3.3 0.0 copy-start
  3.3 1.0 copy-done
  4.3 137.0 %shard_map.46 = bf16[8,8,32,128]{3,2,1,0:T(8,128)(2,1)S(1)} custom-call(bf16[16,8,128,128]{3,2,1,0:T(8,128)(2,1)} %bitcast.13, s32[16,8]{1,0:T(8,128)S(1)} %copy.6.pattern, f32[8,256,128]{2,1,0:T(8,128)} %bitcast.14, f32[8,128,128]{2,1,0:T(8,128)S(1)} %bitcast.12), custom_call_target="tpu_custom_call" | custom-call | tf_op jit(solution)/shard_map/pallas_call | solution.py:466
  141.3 0.1 bitcast_convert_fusion
  141.4 1.3 copy.7
Async XLA Ops:
  3.3 1.0 copy-start

commit v3 on v2

--- a/solution.py
+++ b/solution.py
@@ -85,18 +85,15 @@
 MESH = pl.DeviceIdType.MESH
 NT = (((1,), (1,)), ((), ()))
 NN = (((1,), (0,)), ((), ()))
-HIGHEST = lax.Precision.HIGHEST
-
-
-def dot(a, b, dims, precision=None):
-    return lax.dot_general(
-        a, b, dims, precision=precision, preferred_element_type=jnp.float32
-    )
+
+
+def dot(a, b, dims):
+    return lax.dot_general(a, b, dims, preferred_element_type=jnp.float32)
 
 
 def kernel(
     nz, nc, blk, scen, factor, pattern, loads, inverse, out,
-    near, own, rhs, diag, yval, ylow, yfull, fpart, fsum, xlow, xfull,
+    turned, split, near, own, rhs, diag, yval, ylow, yfull, fpart, fsum, xlow, xfull,
     part, sums, bpart, bsum, landed,
     sib_s, sib_r, chip_s, chip_r,
     load_own, load_s, load_r, diag_own, diag_s, diag_r, diag_sib_s, diag_sib_r,
@@ -114,21 +111,9 @@
     owner = c % nz == z
     relays = core == z % 2
     mine = c // nz
-
-    def remote(src, dst, s, r, to):
-        return pltpu.make_async_remote_copy(
-            src_ref=src, dst_ref=dst, send_sem=s, recv_sem=r, device_id=to, device_id_type=MESH
-        )
-
-    def share(col):
-        return pl.ds(pl.multiple_of(col * width, width), width)
-
-    def masked(row, col):
-        return factor[row, col] * pattern[row, col].astype(jnp.float32).astype(jnp.bfloat16)
-
-    for level in range(1, LEVELS):
-        for g in range(groups):
-            near[c, level, g * blk : (g + 1) * blk] = masked(level * groups + g, level - 1)
+    span = groups * blk
+    place = (c % nz) * groups + c // nz
+    cuts = ((0, 1), (1, 3), (3, LEVELS))
 
     barrier = pltpu.get_barrier_semaphore()
     for step in range(1, nz * nc):
@@ -136,28 +121,84 @@
         pl.semaphore_signal(
             barrier, inc=1, device_id=(other // nc, other % nc), device_id_type=MESH
         )
+
+    def remote(src, dst, s, r, to):
+        return pltpu.make_async_remote_copy(
+            src_ref=src, dst_ref=dst, send_sem=s, recv_sem=r, device_id=to, device_id_type=MESH
+        )
+
+    def share(col):
+        return pl.ds(pl.multiple_of(col * width, width), width)
+
+    def masked(row, col):
+        return factor[row, col] * pattern[row, col].astype(jnp.float32).astype(jnp.bfloat16)
+
+    def lane(index, size):
+        return pl.ds(pl.multiple_of(index * size, size), size)
+
+    def turn(level):
+        turned[level] = loads[level].T
+
+    def halves(value):
+        high = value.astype(jnp.bfloat16)
+        return high, (value - high.astype(jnp.float32)).astype(jnp.bfloat16)
+
+    for level in range(LEVELS):
+        high, rest = halves(inverse[level])
+        split[level, :, :blk] = high
+        split[level, :, blk:] = rest
+    for level in range(1, LEVELS):
+        for g in range(groups):
+            rows = slice(g * blk, (g + 1) * blk)
+            near[level, rows, lane(place, blk)] = masked(level * groups + g, level - 1)
+    turn(0)
     pl.semaphore_wait(barrier, nz * nc - 1)
 
-    def load_copy(step):
+    def load_copy(cut, step):
         to = (c + step) % nc
+        levels = pl.ds(cuts[cut][0], cuts[cut][1] - cuts[cut][0])
         return remote(
-            loads.at[:, share(to), :], rhs.at[mine],
-            load_s.at[step], load_r.at[mine], (z, to),
-        )
-
-    def load_self():
-        return pltpu.make_async_copy(loads.at[:, share(c), :], rhs.at[mine], load_own)
+            turned.at[levels, share(to), :], rhs.at[mine, levels],
+            load_s.at[cut, step], load_r.at[cut, mine], (z, to),
+        )
+
+    def load_self(cut):
+        levels = pl.ds(cuts[cut][0], cuts[cut][1] - cuts[cut][0])
+        return pltpu.make_async_copy(
+            turned.at[levels, share(c), :], rhs.at[mine, levels], load_own.at[cut]
+        )
+
+    def load_start(cut):
+        @pl.when(owner)
+        def _():
+            load_self(cut).start()
+            for step in range(1, nc):
+                load_copy(cut, step).start()
+
+    def load_wait(cut):
+        levels = pl.ds(cuts[cut][0], cuts[cut][1] - cuts[cut][0])
+        for g in range(groups):
+            @pl.when(c != z + nz * g)
+            def _():
+                here = rhs.at[g, levels]
+                remote(
+                    here, here, load_s.at[cut, 0], load_r.at[cut, g], (z, sibling)
+                ).wait_recv()
+
+        @pl.when(owner)
+        def _():
+            load_self(cut).wait()
 
     def diag_copy(level, step):
         to = ((chip + step) % chips) * 2 + core
         return remote(
-            inverse.at[level], diag.at[mine, level],
+            split.at[level], diag.at[mine, level],
             diag_s.at[level, step], diag_r.at[level, mine], (z, to),
         )
 
     def diag_self(level):
         return pltpu.make_async_copy(
-            inverse.at[level], diag.at[mine, level], diag_own.at[level]
+            split.at[level], diag.at[mine, level], diag_own.at[level]
         )
 
     def diag_sib(level, g):
@@ -168,20 +209,15 @@
 
     def chip_copy(level, step):
         to = ((chip + step) % chips) * 2 + core
-        here = near.at[c, level]
+        here = near.at[level, :, lane(place, blk)]
         return remote(here, here, chip_s.at[level, step], chip_r.at[level, step], (z, to))
 
     def sib_copy(level, step):
-        here = near.at[((chip + chips - step) % chips) * 2 + core, level]
+        col = ((chip + chips - step) % chips) * 2 + core
+        here = near.at[level, :, lane((col % nz) * groups + col // nz, blk)]
         return remote(here, here, sib_s.at[level, step], sib_r.at[level, step], (z, sibling))
 
-    @pl.when(owner)
-    def _():
-        load_self().start()
-        for step in range(1, nc):
-            load_copy(step).start()
-
-    for level in range(LEVELS):
+    def spread(level):
         @pl.when(owner)
         def _():
             diag_self(level).start()
@@ -193,10 +229,18 @@
                 chip_copy(level, step).start()
             sib_copy(level, 0).start()
 
+    load_start(0)
+    spread(0)
+    spread(1)
+    for level in range(1, LEVELS):
+        turn(level)
+    load_start(1)
+    spread(2)
     for level in range(2, LEVELS):
         for g in range(groups):
             for col in range(level - 1):
-                own[level * groups + g, col] = masked(level * groups + g, col)
+                block = masked(level * groups + g, col)
+                own[level, g * blk : (g + 1) * blk, col * blk : (col + 1) * blk] = block
 
     def relay(level):
         @pl.when(relays)
@@ -248,17 +292,19 @@
                 sib_copy(level, step).wait_send()
 
     def y_copy(level, step):
-        here = ylow.at[level, z]
+        here = ylow.at[level, :, lane(z, span)]
         return remote(
             here, here, y_s.at[level, step], y_r.at[level, step], ((z + step) % nz, c)
         )
 
-    def to_columns(src, dst, s, r, act):
+    def to_columns(source, dst, s, r, act):
         for g in range(groups):
+            src = source(g)
+
             for step in range(nz):
                 def go():
                     copy = remote(
-                        src.at[g], dst, s.at[step, g], r, ((z + step) % nz, z + nz * g)
+                        src, dst, s.at[step, g], r, ((z + step) % nz, z + nz * g)
                     )
                     copy.start() if act else copy.wait_send()
 
@@ -269,31 +315,33 @@
                     if act:
                         @pl.when(c == z + nz * g)
                         def _():
-                            pltpu.make_async_copy(src.at[g], dst, r).start()
+                            pltpu.make_async_copy(src, dst, r).start()
 
     def y_far(level, act):
         to_columns(
-            ylow.at[level, z], yfull.at[level, share(c), :], yf_s.at[level], yf_r.at[level], act
+            lambda g: ylow.at[level, :, lane(z * groups + g, blk)],
+            yfull.at[share(c), pl.ds(level * blk, blk)],
+            yf_s.at[level], yf_r.at[level], act,
         )
 
     def out_far(level, act):
-        to_columns(xlow.at[level], landed.at[level, c], out_s.at[level], out_r.at[level], act)
+        pair = pl.ds(level, 2)
+        to_columns(
+            lambda g: xlow.at[pair, :, pl.ds(g * blk, blk)], landed.at[pair, c],
+            out_s.at[level], out_r.at[level], act,
+        )
 
     def f_far(level, act):
         for step in range(1, nc):
             to = (c + step) % nc
             copy = remote(
-                fpart.at[level, :, share(to), :], fsum.at[level, c],
+                fpart.at[level, share(to), :], fsum.at[level, step - 1],
                 f_s.at[level, step], f_r.at[level], (z, to),
             )
             copy.start() if act else copy.wait_send()
-        if act:
-            pltpu.make_async_copy(
-                fpart.at[level, :, share(c), :], fsum.at[level, c], f_r.at[level]
-            ).start()
 
     def x_far(level, act):
-        here = xfull.at[level, :, share(c), :]
+        here = xfull.at[level, share(c), :]
         for step in range(1, nc):
             copy = remote(
                 xlow.at[level], here, xf_s.at[level, step], xf_r.at[level], (z, (c + step) % nc)
@@ -305,7 +353,7 @@
     def b_far(level, act):
         for step in range(nc):
             to = (c + step) % nc
-            src, dst = bpart.at[level, share(to), :], bsum.at[level, z, mine]
+            src, dst = bpart.at[level, share(to), :], bsum.at[level, z, :, lane(mine, blk)]
 
             def go():
                 copy = remote(src, dst, b_s.at[level, step], b_r.at[level], (c % nz, to))
@@ -323,52 +371,57 @@
     def all_in(ref, sem):
         pltpu.make_async_copy(ref, ref, sem).wait()
 
+    def apply(value, low, rest, dims):
+        axis = dims[0][1][0]
+        high, small = halves(value)
+        left = jnp.concatenate([high, small, high], axis=1)
+        return dot(left, jnp.concatenate([low, low, rest], axis=axis), dims)
+
+    def solve(level, value, dims):
+        return [
+            apply(
+                value[:, g * blk : (g + 1) * blk],
+                diag[g, level, :, :blk], diag[g, level, :, blk:], dims,
+            )
+            for g in range(groups)
+        ]
+
     relay(0)
-    for g in range(groups):
-        @pl.when(c != z + nz * g)
-        def _():
-            remote(
-                rhs.at[g], rhs.at[g], load_s.at[0], load_r.at[g], (z, sibling)
-            ).wait_recv()
-
-    @pl.when(owner)
-    def _():
-        load_self().wait()
+    load_wait(0)
 
     for level in range(LEVELS):
+        for cut in range(1, len(cuts)):
+            if level == cuts[cut][0]:
+                load_wait(cut)
         arrived(level)
-        resid = [rhs[g, level] for g in range(groups)]
+        resid = jnp.concatenate([rhs[g, level] for g in range(groups)], axis=1)
         if level > 1:
             all_in(fsum.at[level], f_r.at[level])
-            for g in range(groups):
-                for col in range(nc):
-                    resid[g] = resid[g] - fsum[level, col, g].astype(jnp.float32)
+            resid = resid - fpart[level, share(c), :].astype(jnp.float32)
+            for step in range(nc - 1):
+                resid = resid - fsum[level, step].astype(jnp.float32)
         if level > 0:
             for step in range(1, nz):
                 y_copy(level - 1, step).wait_recv()
-            total = jnp.zeros((width, groups * blk), jnp.float32)
-            for col in range(nc):
-                total = total + dot(ylow[level - 1, col % nz, col // nz], near[col, level], NT)
-            resid = [resid[g] - total[:, g * blk : (g + 1) * blk] for g in range(groups)]
-        for g in range(groups):
-            solved = dot(resid[g], diag[g, level], NT, HIGHEST)
-            yval[g, level] = solved
-            if level < last:
-                ylow[level, z, g] = solved.astype(jnp.bfloat16)
+            resid = resid - dot(ylow[level - 1], near[level], NT)
+        solved = jnp.concatenate(solve(level, resid, NT), axis=1)
+        yval[level] = solved
         if level < last:
+            ylow[level, :, lane(z, span)] = solved.astype(jnp.bfloat16)
             for step in range(1, nz):
                 y_copy(level, step).start()
             if level > 0:
-                all_in(yfull.at[level - 1], yf_r.at[level - 1])
-                for g in range(groups):
-                    row = (level + 1) * groups + g
-                    value = dot(yfull[0], own[row, 0], NT)
-                    for col in range(1, level):
-                        value = value + dot(yfull[col], own[row, col], NT)
-                    fpart[level + 1, g] = value.astype(jnp.bfloat16)
+                some = yfull.at[:, pl.ds((level - 1) * blk, blk)]
+                all_in(some, yf_r.at[level - 1])
+                value = dot(yfull[:, : level * blk], own[level + 1, :, : level * blk], NT)
+                fpart[level + 1] = value.astype(jnp.bfloat16)
                 f_far(level + 1, True)
             if level < last - 1:
                 y_far(level, True)
+            if level + 3 < LEVELS:
+                spread(level + 3)
+            if level == 0:
+                load_start(2)
             relay(level + 1)
             if level > 0:
                 for step in range(1, nz):
@@ -381,30 +434,27 @@
     def part_copy(level, step):
         to = (z + step) % nz
         return remote(
-            part.at[level, to], sums.at[level, z],
+            part.at[level, :, lane(to, span)], sums.at[level, step - 1],
             p_s.at[level, step], p_r.at[level, step], (to, c),
         )
 
     for level in reversed(range(LEVELS)):
         if level < last:
-            above = jnp.concatenate([xlow[level + 1, g] for g in range(groups)], axis=1)
-            for col in range(nc):
-                value = dot(above, near[col, level + 1], NN)
-                part[level, col % nz, col // nz] = value.astype(jnp.bfloat16)
+            part[level] = dot(xlow[level + 1], near[level + 1], NN).astype(jnp.bfloat16)
             for step in range(1, nz):
                 part_copy(level, step).start()
             if level < last - 1:
                 all_in(xfull.at[level + 2], xf_r.at[level + 2])
                 value = None
                 for up in range(level + 2, LEVELS):
-                    for g in range(groups):
-                        term = dot(xfull[up, g], own[up * groups + g, level], NN)
-                        value = term if value is None else value + term
+                    term = dot(xfull[up], own[up, :, level * blk : (level + 1) * blk], NN)
+                    value = term if value is None else value + term
                 bpart[level] = value.astype(jnp.bfloat16)
                 b_far(level, True)
             if level > 0:
                 x_far(level + 1, True)
-            out_far(level + 1, True)
+            if level % 2 == 1:
+                out_far(level + 1, True)
             if level == last - 1:
                 for step in range(1, nz):
                     y_copy(last - 1, step).wait_send()
@@ -414,43 +464,41 @@
 
                 @pl.when(owner)
                 def _():
-                    for step in range(1, nc):
-                        load_copy(step).wait_send()
+                    for cut in range(len(cuts)):
+                        for step in range(1, nc):
+                            load_copy(cut, step).wait_send()
             else:
                 for step in range(1, nz):
                     part_copy(level + 1, step).wait_send()
                 x_far(level + 2, False)
+            if level % 2 == 0 and level < last - 1:
                 out_far(level + 2, False)
-                all_in(landed.at[level + 2], out_r.at[level + 2])
+                pair = landed.at[pl.ds(level + 2, 2)]
+                all_in(pair, out_r.at[level + 2])
+                out[level + 2 : level + 4] = landed[level + 2 : level + 4]
             if level < last - 2:
                 b_far(level + 1, False)
             for step in range(1, nz):
                 part_copy(level, step).wait_recv()
-            if level < last - 1:
-                all_in(bsum.at[level], b_r.at[level])
-        for g in range(groups):
-            resid = yval[g, level]
-            if level < last:
-                for step in range(nz):
-                    if step == 0:
-                        piece = part[level, z, g]
-                    else:
-                        piece = sums[level, (z + nz - step) % nz, g]
-                    resid = resid - piece.astype(jnp.float32)
-                    if level < last - 1:
-                        resid = resid - bsum[level, step, g].astype(jnp.float32)
-            xlow[level, g] = dot(resid, diag[g, level], NN, HIGHEST).astype(jnp.bfloat16)
+        resid = yval[level]
+        if level < last:
+            resid = resid - part[level, :, lane(z, span)].astype(jnp.float32)
+            for step in range(1, nz):
+                resid = resid - sums[level, step - 1].astype(jnp.float32)
+        if level < last - 1:
+            all_in(bsum.at[level], b_r.at[level])
+            for step in range(nz):
+                resid = resid - bsum[level, step].astype(jnp.float32)
+        solved = jnp.concatenate(solve(level, resid, NN), axis=1)
+        xlow[level] = solved.astype(jnp.bfloat16)
 
     out_far(0, True)
     for step in range(1, nz):
         part_copy(0, step).wait_send()
     b_far(0, False)
-    out_far(1, False)
-    all_in(landed.at[1], out_r.at[1])
-    out[1:] = landed[1:]
     out_far(0, False)
-    all_in(landed.at[0], out_r.at[0])
-    out[0] = landed[0]
+    all_in(landed.at[pl.ds(0, 2)], out_r.at[0])
+    out[0:2] = landed[0:2]
 
 
 def split_plan(factor, pattern, loads, block_inverse):
@@ -458,7 +506,7 @@
     rows, cols, blk = factor.shape[0], factor.shape[2], factor.shape[4]
     scen = loads.shape[3]
     groups, chips, width = nc // nz, nc // 2, scen // nc
-    turned = jnp.swapaxes(loads[:, 0], 1, 2)
+    span = groups * blk
     low, f32 = jnp.bfloat16, jnp.float32
     dma = pltpu.SemaphoreType.DMA
     vmem = pl.BlockSpec(memory_space=pltpu.VMEM)
@@ -469,25 +517,27 @@
         in_specs=[vmem, smem, vmem, vmem],
         out_specs=vmem,
         scratch_shapes=[
-            pltpu.VMEM((nc, LEVELS, groups * blk, blk), low),
-            pltpu.VMEM((rows, cols, blk, blk), low),
+            pltpu.VMEM((LEVELS, scen, blk), f32),
+            pltpu.VMEM((LEVELS, blk, 2 * blk), low),
+            pltpu.VMEM((LEVELS, span, nc * blk), low),
+            pltpu.VMEM((LEVELS, span, cols * blk), low),
             pltpu.VMEM((groups, LEVELS, width, blk), f32),
-            pltpu.VMEM((groups, LEVELS, blk, blk), f32),
-            pltpu.VMEM((groups, LEVELS, width, blk), f32),
-            pltpu.VMEM((LEVELS, nz, groups, width, blk), low),
+            pltpu.VMEM((groups, LEVELS, blk, 2 * blk), low),
+            pltpu.VMEM((LEVELS, width, span), f32),
+            pltpu.VMEM((LEVELS, width, nc * blk), low),
+            pltpu.VMEM((scen, LEVELS * blk), low),
+            pltpu.VMEM((LEVELS, scen, span), low),
+            pltpu.VMEM((LEVELS, nc - 1, width, span), low),
+            pltpu.VMEM((LEVELS, width, span), low),
+            pltpu.VMEM((LEVELS, scen, span), low),
+            pltpu.VMEM((LEVELS, width, nc * blk), low),
+            pltpu.VMEM((LEVELS, nz - 1, width, span), low),
             pltpu.VMEM((LEVELS, scen, blk), low),
-            pltpu.VMEM((LEVELS, groups, scen, blk), low),
-            pltpu.VMEM((LEVELS, nc, groups, width, blk), low),
-            pltpu.VMEM((LEVELS, groups, width, blk), low),
-            pltpu.VMEM((LEVELS, groups, scen, blk), low),
-            pltpu.VMEM((LEVELS, nz, groups, width, blk), low),
-            pltpu.VMEM((LEVELS, nz, groups, width, blk), low),
-            pltpu.VMEM((LEVELS, scen, blk), low),
-            pltpu.VMEM((LEVELS, nz, groups, width, blk), low),
+            pltpu.VMEM((LEVELS, nz, width, span), low),
             pltpu.VMEM((LEVELS, nc, width, blk), low),
             dma((LEVELS, chips)), dma((LEVELS, chips)),
             dma((LEVELS, chips)), dma((LEVELS, chips)),
-            dma, dma((nc,)), dma((groups,)),
+            dma((3,)), dma((3, nc)), dma((3, groups)),
             dma((LEVELS,)), dma((LEVELS, chips)), dma((LEVELS, groups)),
             dma((LEVELS, groups)), dma((LEVELS, groups)),
             dma((LEVELS, nz)), dma((LEVELS, nz)),
@@ -501,7 +551,7 @@
         compiler_params=pltpu.CompilerParams(
             collective_id=0, has_side_effects=True, vmem_limit_bytes=52 * 2**20
         ),
-    )(factor[:, 0, :, 0], pattern[:, 0, :, 0], turned, block_inverse[:, 0])
+    )(factor[:, 0, :, 0], pattern[:, 0, :, 0], loads[:, 0], block_inverse[:, 0])
     result = result.reshape(LEVELS, scen, blk).astype(f32)
     return jnp.swapaxes(result, 1, 2)[:, None]
 

time: 143 us -> 128 us (0.90)
  Pallas kernels: 137 us -> 124 us
  local copies, waits for them, and re-layouts: 5.63 us -> 3.11 us
    pallas_call x1, Pallas kernels: 137 us -> 124 us  [split_plan(): pl.pallas_call(functools.partial(kernel, nz, nc, blk, scen), out_shape=ja...]
    unnamed x3 -> x2, local copies, waits for them, and re-layouts: 3.57 us -> 1.04 us
where the time goes in v3:
time: 128 us
  Pallas kernels  124 us (97%)
  local copies, waits for them, and re-layouts  3.11 us (2%)
    pallas_call x1, Pallas kernels, split_plan(): pl.pallas_call(functools.partial(kernel, nz, nc, blk, scen), out_shape=ja...  124 us

profile of v3, /device:TPU:0, one launch (start us, length us, event | category | flops | bytes accessed | tf_op | source)
XLA Modules:
  0.0 127.5 jit_solution(7291145925921444866)
XLA Ops:
  0.0 0.8 copy.5.pattern
  0.8 0.0 copy-start
  0.8 1.0 copy-done
  1.8 124.3 %shard_map.46 = bf16[8,8,32,128]{3,2,1,0:T(8,128)(2,1)S(1)} custom-call(bf16[16,8,128,128]{3,2,1,0:T(8,128)(2,1)} %bitcast.11, s32[16,8]{1,0:T(8,128)S(1)} %copy.5.pattern, f32[8,128,256]{2,1,0:T(8,128)} %bitcast.12, f32[8,128,128]{2,1,0:T(8,128)S(1)} %bitcast.10), custom_call_target="tpu_custom_call" | custom-call | tf_op jit(solution)/shard_map/pallas_call | solution.py:514
  126.1 0.1 bitcast_convert_fusion
  126.2 1.3 %copy.6 = f32[8,256,128]{1,2,0:T(8,128)} copy(f32[8,256,128]{2,1,0:T(8,128)S(1)} %bitcast_convert_fusion) | data formatting | bytes 2097152 | tf_op jit(solution)/shard_map/broadcast_in_dim | solution.py:556
Async XLA Ops:
  0.8 1.0 copy-start

commit v4 on v3

--- a/solution.py
+++ b/solution.py
@@ -143,15 +143,18 @@
         high = value.astype(jnp.bfloat16)
         return high, (value - high.astype(jnp.float32)).astype(jnp.bfloat16)
 
-    for level in range(LEVELS):
+    def prepare(level):
         high, rest = halves(inverse[level])
         split[level, :, :blk] = high
         split[level, :, blk:] = rest
-    for level in range(1, LEVELS):
-        for g in range(groups):
-            rows = slice(g * blk, (g + 1) * blk)
-            near[level, rows, lane(place, blk)] = masked(level * groups + g, level - 1)
+        if level > 0:
+            for g in range(groups):
+                rows = slice(g * blk, (g + 1) * blk)
+                near[level, rows, lane(place, blk)] = masked(level * groups + g, level - 1)
+
+    prepare(0)
     turn(0)
+    prepare(1)
     pl.semaphore_wait(barrier, nz * nc - 1)
 
     def load_copy(cut, step):
@@ -235,7 +238,10 @@
     for level in range(1, LEVELS):
         turn(level)
     load_start(1)
+    prepare(2)
     spread(2)
+    for level in range(3, LEVELS):
+        prepare(level)
     for level in range(2, LEVELS):
         for g in range(groups):
             for col in range(level - 1):
@@ -318,11 +324,15 @@
                             pltpu.make_async_copy(src, dst, r).start()
 
     def y_far(level, act):
-        to_columns(
-            lambda g: ylow.at[level, :, lane(z * groups + g, blk)],
-            yfull.at[share(c), pl.ds(level * blk, blk)],
-            yf_s.at[level], yf_r.at[level], act,
-        )
+        here = yfull.at[share(c), pl.ds(level * blk, blk)]
+        for step in range(nc):
+            to = (c + step) % nc
+            src = ylow.at[level, :, lane((to % nz) * groups + to // nz, blk)]
+            if step > 0:
+                copy = remote(src, here, yf_s.at[level, step], yf_r.at[level], (z, to))
+                copy.start() if act else copy.wait_send()
+            elif act:
+                pltpu.make_async_copy(src, here, yf_r.at[level]).start()
 
     def out_far(level, act):
         pair = pl.ds(level, 2)
@@ -351,22 +361,15 @@
             pltpu.make_async_copy(xlow.at[level], here, xf_r.at[level]).start()
 
     def b_far(level, act):
+        here = bsum.at[level, :, lane(place, blk)]
         for step in range(nc):
             to = (c + step) % nc
-            src, dst = bpart.at[level, share(to), :], bsum.at[level, z, :, lane(mine, blk)]
-
-            def go():
-                copy = remote(src, dst, b_s.at[level, step], b_r.at[level], (c % nz, to))
+            src = bpart.at[level, share(to), :]
+            if step > 0:
+                copy = remote(src, here, b_s.at[level, step], b_r.at[level], (z, to))
                 copy.start() if act else copy.wait_send()
-
-            if step > 0:
-                go()
-            else:
-                pl.when(jnp.logical_not(owner))(go)
-                if act:
-                    @pl.when(owner)
-                    def _():
-                        pltpu.make_async_copy(src, dst, b_r.at[level]).start()
+            elif act:
+                pltpu.make_async_copy(src, here, b_r.at[level]).start()
 
     def all_in(ref, sem):
         pltpu.make_async_copy(ref, ref, sem).wait()
@@ -395,15 +398,17 @@
                 load_wait(cut)
         arrived(level)
         resid = jnp.concatenate([rhs[g, level] for g in range(groups)], axis=1)
-        if level > 1:
-            all_in(fsum.at[level], f_r.at[level])
-            resid = resid - fpart[level, share(c), :].astype(jnp.float32)
-            for step in range(nc - 1):
-                resid = resid - fsum[level, step].astype(jnp.float32)
         if level > 0:
             for step in range(1, nz):
                 y_copy(level - 1, step).wait_recv()
+            if level < last:
+                y_far(level - 1, True)
             resid = resid - dot(ylow[level - 1], near[level], NT)
+        if level > 1:
+            resid = resid - fpart[level, share(c), :].astype(jnp.float32)
+            all_in(fsum.at[level], f_r.at[level])
+            for step in range(nc - 1):
+                resid = resid - fsum[level, step].astype(jnp.float32)
         solved = jnp.concatenate(solve(level, resid, NT), axis=1)
         yval[level] = solved
         if level < last:
@@ -411,13 +416,16 @@
             for step in range(1, nz):
                 y_copy(level, step).start()
             if level > 0:
-                some = yfull.at[:, pl.ds((level - 1) * blk, blk)]
-                all_in(some, yf_r.at[level - 1])
-                value = dot(yfull[:, : level * blk], own[level + 1, :, : level * blk], NT)
+                value = None
+                if level > 1:
+                    done = slice(0, (level - 1) * blk)
+                    value = dot(yfull[:, done], own[level + 1, :, done], NT)
+                fresh = slice((level - 1) * blk, level * blk)
+                all_in(yfull.at[:, pl.ds((level - 1) * blk, blk)], yf_r.at[level - 1])
+                term = dot(yfull[:, fresh], own[level + 1, :, fresh], NT)
+                value = term if value is None else value + term
                 fpart[level + 1] = value.astype(jnp.bfloat16)
                 f_far(level + 1, True)
-            if level < last - 1:
-                y_far(level, True)
             if level + 3 < LEVELS:
                 spread(level + 3)
             if level == 0:
@@ -440,17 +448,13 @@
 
     for level in reversed(range(LEVELS)):
         if level < last:
-            part[level] = dot(xlow[level + 1], near[level + 1], NN).astype(jnp.bfloat16)
+            value = dot(xlow[level + 1], near[level + 1], NN)
+            if level < last - 1:
+                all_in(bsum.at[level], b_r.at[level])
+                value = value + bsum[level].astype(jnp.float32)
+            part[level] = value.astype(jnp.bfloat16)
             for step in range(1, nz):
                 part_copy(level, step).start()
-            if level < last - 1:
-                all_in(xfull.at[level + 2], xf_r.at[level + 2])
-                value = None
-                for up in range(level + 2, LEVELS):
-                    term = dot(xfull[up], own[up, :, level * blk : (level + 1) * blk], NN)
-                    value = term if value is None else value + term
-                bpart[level] = value.astype(jnp.bfloat16)
-                b_far(level, True)
             if level > 0:
                 x_far(level + 1, True)
             if level % 2 == 1:
@@ -476,8 +480,18 @@
                 pair = landed.at[pl.ds(level + 2, 2)]
                 all_in(pair, out_r.at[level + 2])
                 out[level + 2 : level + 4] = landed[level + 2 : level + 4]
-            if level < last - 2:
-                b_far(level + 1, False)
+            if level > 0:
+                value = None
+                lanes = slice((level - 1) * blk, level * blk)
+                for up in reversed(range(level + 1, LEVELS)):
+                    if up == level + 1:
+                        all_in(xfull.at[up], xf_r.at[up])
+                    term = dot(xfull[up], own[up, :, lanes], NN)
+                    value = term if value is None else value + term
+                bpart[level - 1] = value.astype(jnp.bfloat16)
+                b_far(level - 1, True)
+            if level < last - 1:
+                b_far(level, False)
             for step in range(1, nz):
                 part_copy(level, step).wait_recv()
         resid = yval[level]
@@ -485,17 +499,12 @@
             resid = resid - part[level, :, lane(z, span)].astype(jnp.float32)
             for step in range(1, nz):
                 resid = resid - sums[level, step - 1].astype(jnp.float32)
-        if level < last - 1:
-            all_in(bsum.at[level], b_r.at[level])
-            for step in range(nz):
-                resid = resid - bsum[level, step].astype(jnp.float32)
         solved = jnp.concatenate(solve(level, resid, NN), axis=1)
         xlow[level] = solved.astype(jnp.bfloat16)
 
     out_far(0, True)
     for step in range(1, nz):
         part_copy(0, step).wait_send()
-    b_far(0, False)
     out_far(0, False)
     all_in(landed.at[pl.ds(0, 2)], out_r.at[0])
     out[0:2] = landed[0:2]
@@ -533,7 +542,7 @@
             pltpu.VMEM((LEVELS, width, nc * blk), low),
             pltpu.VMEM((LEVELS, nz - 1, width, span), low),
             pltpu.VMEM((LEVELS, scen, blk), low),
-            pltpu.VMEM((LEVELS, nz, width, span), low),
+            pltpu.VMEM((LEVELS, width, nc * blk), low),
             pltpu.VMEM((LEVELS, nc, width, blk), low),
             dma((LEVELS, chips)), dma((LEVELS, chips)),
             dma((LEVELS, chips)), dma((LEVELS, chips)),
@@ -541,7 +550,7 @@
             dma((LEVELS,)), dma((LEVELS, chips)), dma((LEVELS, groups)),
             dma((LEVELS, groups)), dma((LEVELS, groups)),
             dma((LEVELS, nz)), dma((LEVELS, nz)),
-            dma((LEVELS, nz, groups)), dma((LEVELS,)),
+            dma((LEVELS, nc)), dma((LEVELS,)),
             dma((LEVELS, nc)), dma((LEVELS,)),
             dma((LEVELS, nz)), dma((LEVELS, nz)),
             dma((LEVELS, nc)), dma((LEVELS,)),

time: 128 us -> 138 us (1.078)
  Pallas kernels: 124 us -> 134 us
    pallas_call x1, Pallas kernels: 124 us -> 134 us  [split_plan(): pl.pallas_call(functools.partial(kernel, nz, nc, blk, scen), out_shape=ja...]
where the time goes in v4:
time: 138 us
  Pallas kernels  134 us (97%)
  local copies, waits for them, and re-layouts  3.11 us (2%)
    pallas_call x1, Pallas kernels, split_plan(): pl.pallas_call(functools.partial(kernel, nz, nc, blk, scen), out_shape=ja...  134 us

profile of v4, /device:TPU:0, one launch (start us, length us, event | category | flops | bytes accessed | tf_op | source)
XLA Modules:
  0.0 137.5 jit_solution(1828057355310827689)
XLA Ops:
  0.0 0.8 copy.5.pattern
  0.8 0.0 copy-start
  0.8 1.0 copy-done
  1.8 134.3 %shard_map.46 = bf16[8,8,32,128]{3,2,1,0:T(8,128)(2,1)S(1)} custom-call(bf16[16,8,128,128]{3,2,1,0:T(8,128)(2,1)} %bitcast.11, s32[16,8]{1,0:T(8,128)S(1)} %copy.5.pattern, f32[8,128,256]{2,1,0:T(8,128)} %bitcast.12, f32[8,128,128]{2,1,0:T(8,128)S(1)} %bitcast.10), custom_call_target="tpu_custom_call" | custom-call | tf_op jit(solution)/shard_map/pallas_call | solution.py:523
  136.1 0.1 bitcast_convert_fusion
  136.2 1.3 copy.6
Async XLA Ops:
  0.8 1.0 copy-start

commit v5 on v4

--- a/solution.py
+++ b/solution.py
@@ -324,15 +324,11 @@
                             pltpu.make_async_copy(src, dst, r).start()
 
     def y_far(level, act):
-        here = yfull.at[share(c), pl.ds(level * blk, blk)]
-        for step in range(nc):
-            to = (c + step) % nc
-            src = ylow.at[level, :, lane((to % nz) * groups + to // nz, blk)]
-            if step > 0:
-                copy = remote(src, here, yf_s.at[level, step], yf_r.at[level], (z, to))
-                copy.start() if act else copy.wait_send()
-            elif act:
-                pltpu.make_async_copy(src, here, yf_r.at[level]).start()
+        to_columns(
+            lambda g: ylow.at[level, :, lane(z * groups + g, blk)],
+            yfull.at[share(c), pl.ds(level * blk, blk)],
+            yf_s.at[level], yf_r.at[level], act,
+        )
 
     def out_far(level, act):
         pair = pl.ds(level, 2)
@@ -361,15 +357,22 @@
             pltpu.make_async_copy(xlow.at[level], here, xf_r.at[level]).start()
 
     def b_far(level, act):
-        here = bsum.at[level, :, lane(place, blk)]
         for step in range(nc):
             to = (c + step) % nc
-            src = bpart.at[level, share(to), :]
+            src, dst = bpart.at[level, share(to), :], bsum.at[level, z, :, lane(mine, blk)]
+
+            def go():
+                copy = remote(src, dst, b_s.at[level, step], b_r.at[level], (c % nz, to))
+                copy.start() if act else copy.wait_send()
+
             if step > 0:
-                copy = remote(src, here, b_s.at[level, step], b_r.at[level], (z, to))
-                copy.start() if act else copy.wait_send()
-            elif act:
-                pltpu.make_async_copy(src, here, b_r.at[level]).start()
+                go()
+            else:
+                pl.when(jnp.logical_not(owner))(go)
+                if act:
+                    @pl.when(owner)
+                    def _():
+                        pltpu.make_async_copy(src, dst, b_r.at[level]).start()
 
     def all_in(ref, sem):
         pltpu.make_async_copy(ref, ref, sem).wait()
@@ -401,8 +404,6 @@
         if level > 0:
             for step in range(1, nz):
                 y_copy(level - 1, step).wait_recv()
-            if level < last:
-                y_far(level - 1, True)
             resid = resid - dot(ylow[level - 1], near[level], NT)
         if level > 1:
             resid = resid - fpart[level, share(c), :].astype(jnp.float32)
@@ -415,6 +416,8 @@
             ylow[level, :, lane(z, span)] = solved.astype(jnp.bfloat16)
             for step in range(1, nz):
                 y_copy(level, step).start()
+            if level < last - 1:
+                y_far(level, True)
             if level > 0:
                 value = None
                 if level > 1:
@@ -431,13 +434,6 @@
             if level == 0:
                 load_start(2)
             relay(level + 1)
-            if level > 0:
-                for step in range(1, nz):
-                    y_copy(level - 1, step).wait_send()
-                y_far(level - 1, False)
-                spread_sent(level - 1)
-            if level > 1:
-                f_far(level, False)
 
     def part_copy(level, step):
         to = (z + step) % nz
@@ -449,38 +445,11 @@
     for level in reversed(range(LEVELS)):
         if level < last:
             value = dot(xlow[level + 1], near[level + 1], NN)
-            if level < last - 1:
-                all_in(bsum.at[level], b_r.at[level])
-                value = value + bsum[level].astype(jnp.float32)
             part[level] = value.astype(jnp.bfloat16)
             for step in range(1, nz):
                 part_copy(level, step).start()
             if level > 0:
                 x_far(level + 1, True)
-            if level % 2 == 1:
-                out_far(level + 1, True)
-            if level == last - 1:
-                for step in range(1, nz):
-                    y_copy(last - 1, step).wait_send()
-                f_far(last, False)
-                spread_sent(last - 1)
-                spread_sent(last)
-
-                @pl.when(owner)
-                def _():
-                    for cut in range(len(cuts)):
-                        for step in range(1, nc):
-                            load_copy(cut, step).wait_send()
-            else:
-                for step in range(1, nz):
-                    part_copy(level + 1, step).wait_send()
-                x_far(level + 2, False)
-            if level % 2 == 0 and level < last - 1:
-                out_far(level + 2, False)
-                pair = landed.at[pl.ds(level + 2, 2)]
-                all_in(pair, out_r.at[level + 2])
-                out[level + 2 : level + 4] = landed[level + 2 : level + 4]
-            if level > 0:
                 value = None
                 lanes = slice((level - 1) * blk, level * blk)
                 for up in reversed(range(level + 1, LEVELS)):
@@ -490,24 +459,45 @@
                     value = term if value is None else value + term
                 bpart[level - 1] = value.astype(jnp.bfloat16)
                 b_far(level - 1, True)
-            if level < last - 1:
-                b_far(level, False)
-            for step in range(1, nz):
-                part_copy(level, step).wait_recv()
+            if level % 2 == 1:
+                out_far(level + 1, True)
         resid = yval[level]
         if level < last:
             resid = resid - part[level, :, lane(z, span)].astype(jnp.float32)
+        if level < last - 1:
+            all_in(bsum.at[level], b_r.at[level])
+            for step in range(nz):
+                resid = resid - bsum[level, step].astype(jnp.float32)
+        if level < last:
             for step in range(1, nz):
+                part_copy(level, step).wait_recv()
                 resid = resid - sums[level, step - 1].astype(jnp.float32)
         solved = jnp.concatenate(solve(level, resid, NN), axis=1)
         xlow[level] = solved.astype(jnp.bfloat16)
 
     out_far(0, True)
-    for step in range(1, nz):
-        part_copy(0, step).wait_send()
-    out_far(0, False)
-    all_in(landed.at[pl.ds(0, 2)], out_r.at[0])
-    out[0:2] = landed[0:2]
+    for level in range(last):
+        for step in range(1, nz):
+            y_copy(level, step).wait_send()
+            part_copy(level, step).wait_send()
+        if level < last - 1:
+            y_far(level, False)
+            b_far(level, False)
+            f_far(level + 2, False)
+            x_far(level + 2, False)
+    for level in range(LEVELS):
+        spread_sent(level)
+
+    @pl.when(owner)
+    def _():
+        for cut in range(len(cuts)):
+            for step in range(1, nc):
+                load_copy(cut, step).wait_send()
+
+    for level in reversed(range(0, LEVELS, 2)):
+        out_far(level, False)
+        all_in(landed.at[pl.ds(level, 2)], out_r.at[level])
+        out[level : level + 2] = landed[level : level + 2]
 
 
 def split_plan(factor, pattern, loads, block_inverse):
@@ -542,7 +532,7 @@
             pltpu.VMEM((LEVELS, width, nc * blk), low),
             pltpu.VMEM((LEVELS, nz - 1, width, span), low),
             pltpu.VMEM((LEVELS, scen, blk), low),
-            pltpu.VMEM((LEVELS, width, nc * blk), low),
+            pltpu.VMEM((LEVELS, nz, width, span), low),
             pltpu.VMEM((LEVELS, nc, width, blk), low),
             dma((LEVELS, chips)), dma((LEVELS, chips)),
             dma((LEVELS, chips)), dma((LEVELS, chips)),
@@ -550,7 +540,7 @@
             dma((LEVELS,)), dma((LEVELS, chips)), dma((LEVELS, groups)),
             dma((LEVELS, groups)), dma((LEVELS, groups)),
             dma((LEVELS, nz)), dma((LEVELS, nz)),
-            dma((LEVELS, nc)), dma((LEVELS,)),
+            dma((LEVELS, nz, groups)), dma((LEVELS,)),
             dma((LEVELS, nc)), dma((LEVELS,)),
             dma((LEVELS, nz)), dma((LEVELS, nz)),
             dma((LEVELS, nc)), dma((LEVELS,)),

time: 138 us -> 127 us (0.920)
  Pallas kernels: 134 us -> 124 us
    pallas_call x1, Pallas kernels: 134 us -> 124 us  [split_plan(): pl.pallas_call(functools.partial(kernel, nz, nc, blk, scen), out_shape=ja...]
where the time goes in v5:
time: 127 us
  Pallas kernels  124 us (98%)
  local copies, waits for them, and re-layouts  3.11 us (2%)
    pallas_call x1, Pallas kernels, split_plan(): pl.pallas_call(functools.partial(kernel, nz, nc, blk, scen), out_shape=ja...  124 us

profile of v5, /device:TPU:0, one launch (start us, length us, event | category | flops | bytes accessed | tf_op | source)
XLA Modules:
  0.0 127.2 jit_solution(2432623201263250551)
XLA Ops:
  0.0 0.8 copy.5.pattern
  0.8 0.0 copy-start
  0.8 1.0 copy-done
  1.8 124.0 %shard_map.46 = bf16[8,8,32,128]{3,2,1,0:T(8,128)(2,1)S(1)} custom-call(bf16[16,8,128,128]{3,2,1,0:T(8,128)(2,1)} %bitcast.11, s32[16,8]{1,0:T(8,128)S(1)} %copy.5.pattern, f32[8,128,256]{2,1,0:T(8,128)} %bitcast.12, f32[8,128,128]{2,1,0:T(8,128)S(1)} %bitcast.10), custom_call_target="tpu_custom_call" | custom-call | tf_op jit(solution)/shard_map/pallas_call | solution.py:513
  125.8 0.1 bitcast_convert_fusion
  125.9 1.3 %copy.6 = f32[8,256,128]{1,2,0:T(8,128)} copy(f32[8,256,128]{2,1,0:T(8,128)S(1)} %bitcast_convert_fusion) | data formatting | bytes 2097152 | tf_op jit(solution)/shard_map/broadcast_in_dim | solution.py:555
Async XLA Ops:
  0.8 1.0 copy-start

commit v6 on v5

--- a/solution.py
+++ b/solution.py
@@ -109,10 +109,18 @@
     core = c % 2
     sibling = chip * 2 + 1 - core
     owner = c % nz == z
+    leads = [c == z + nz * g for g in range(nc // nz)]
+    trails = [c != z + nz * g for g in range(nc // nz)]
     relays = core == z % 2
     mine = c // nz
     span = groups * blk
-    place = (c % nz) * groups + c // nz
+    rank = (z % 2) * (nz // 2) + z // 2
+    cols = [c] + [(c + step) % nc for step in range(1, nc)]
+    rows_z = [z] + [(z + step) % nz for step in range(1, nz)]
+    ranks = [rank] + [(to % 2) * (nz // 2) + to // 2 for to in rows_z[1:]]
+    peers = [c] + [((chip + step) % chips) * 2 + core for step in range(1, chips)]
+    home = c % nz
+    place = ((home % 2) * (nz // 2) + home // 2) * groups + mine
     cuts = ((0, 1), (1, 3), (3, LEVELS))
 
     barrier = pltpu.get_barrier_semaphore()
@@ -158,7 +166,7 @@
     pl.semaphore_wait(barrier, nz * nc - 1)
 
     def load_copy(cut, step):
-        to = (c + step) % nc
+        to = cols[step]
         levels = pl.ds(cuts[cut][0], cuts[cut][1] - cuts[cut][0])
         return remote(
             turned.at[levels, share(to), :], rhs.at[mine, levels],
@@ -181,7 +189,7 @@
     def load_wait(cut):
         levels = pl.ds(cuts[cut][0], cuts[cut][1] - cuts[cut][0])
         for g in range(groups):
-            @pl.when(c != z + nz * g)
+            @pl.when(trails[g])
             def _():
                 here = rhs.at[g, levels]
                 remote(
@@ -193,32 +201,29 @@
             load_self(cut).wait()
 
     def diag_copy(level, step):
-        to = ((chip + step) % chips) * 2 + core
+        to = peers[step]
         return remote(
-            split.at[level], diag.at[mine, level],
+            split.at[level], diag.at[level, mine],
             diag_s.at[level, step], diag_r.at[level, mine], (z, to),
         )
 
     def diag_self(level):
         return pltpu.make_async_copy(
-            split.at[level], diag.at[mine, level], diag_own.at[level]
-        )
-
-    def diag_sib(level, g):
-        return remote(
-            diag.at[g, level], diag.at[g, level],
-            diag_sib_s.at[level, g], diag_sib_r.at[level, g], (z, sibling),
-        )
+            split.at[level], diag.at[level, mine], diag_own.at[level]
+        )
+
+    def diag_sib(level):
+        here = diag.at[level]
+        return remote(here, here, diag_sib_s.at[level], diag_sib_r.at[level], (z, sibling))
 
     def chip_copy(level, step):
-        to = ((chip + step) % chips) * 2 + core
+        to = peers[step]
         here = near.at[level, :, lane(place, blk)]
         return remote(here, here, chip_s.at[level, step], chip_r.at[level, step], (z, to))
 
-    def sib_copy(level, step):
-        col = ((chip + chips - step) % chips) * 2 + core
-        here = near.at[level, :, lane((col % nz) * groups + col // nz, blk)]
-        return remote(here, here, sib_s.at[level, step], sib_r.at[level, step], (z, sibling))
+    def sib_copy(level):
+        here = near.at[level, :, lane(core, nc // 2 * blk)]
+        return remote(here, here, sib_s.at[level], sib_r.at[level], (z, sibling))
 
     def spread(level):
         @pl.when(owner)
@@ -230,7 +235,6 @@
         if level > 0:
             for step in range(1, chips):
                 chip_copy(level, step).start()
-            sib_copy(level, 0).start()
 
     load_start(0)
     spread(0)
@@ -252,33 +256,31 @@
         @pl.when(relays)
         def _():
             for g in range(groups):
-                @pl.when(c == z + nz * g)
+                @pl.when(leads[g])
                 def _():
                     diag_self(level).wait()
 
-                @pl.when(c != z + nz * g)
+                @pl.when(trails[g])
                 def _():
                     remote(
-                        diag.at[g, level], diag.at[g, level], diag_s.at[level, 0],
+                        diag.at[level, g], diag.at[level, g], diag_s.at[level, 0],
                         diag_r.at[level, g], (z, sibling),
                     ).wait_recv()
 
-                diag_sib(level, g).start()
+            diag_sib(level).start()
 
         if level > 0:
             for step in range(1, chips):
                 chip_copy(level, step).wait_recv()
-                sib_copy(level, step).start()
+            sib_copy(level).start()
 
     def arrived(level):
         @pl.when(jnp.logical_not(relays))
         def _():
-            for g in range(groups):
-                diag_sib(level, g).wait_recv()
+            diag_sib(level).wait_recv()
 
         if level > 0:
-            for step in range(chips):
-                sib_copy(level, step).wait_recv()
+            sib_copy(level).wait_recv()
 
     def spread_sent(level):
         @pl.when(owner)
@@ -288,19 +290,17 @@
 
         @pl.when(relays)
         def _():
-            for g in range(groups):
-                diag_sib(level, g).wait_send()
+            diag_sib(level).wait_send()
 
         if level > 0:
             for step in range(1, chips):
                 chip_copy(level, step).wait_send()
-            for step in range(chips):
-                sib_copy(level, step).wait_send()
+            sib_copy(level).wait_send()
 
     def y_copy(level, step):
-        here = ylow.at[level, :, lane(z, span)]
+        here = ylow.at[level, :, lane(rank, span)]
         return remote(
-            here, here, y_s.at[level, step], y_r.at[level, step], ((z + step) % nz, c)
+            here, here, y_s.at[level, step], y_r.at[level, step], (rows_z[step], c)
         )
 
     def to_columns(source, dst, s, r, act):
@@ -310,28 +310,30 @@
             for step in range(nz):
                 def go():
                     copy = remote(
-                        src, dst, s.at[step, g], r, ((z + step) % nz, z + nz * g)
+                        src, dst, s.at[step, g], r, (rows_z[step], z + nz * g)
                     )
                     copy.start() if act else copy.wait_send()
 
                 if step > 0:
                     go()
                 else:
-                    pl.when(c != z + nz * g)(go)
+                    pl.when(trails[g])(go)
                     if act:
-                        @pl.when(c == z + nz * g)
+                        @pl.when(leads[g])
                         def _():
                             pltpu.make_async_copy(src, dst, r).start()
 
     def y_far(level, act):
         to_columns(
-            lambda g: ylow.at[level, :, lane(z * groups + g, blk)],
+            lambda g: ylow.at[level, :, lane(rank * groups + g, blk)],
             yfull.at[share(c), pl.ds(level * blk, blk)],
             yf_s.at[level], yf_r.at[level], act,
         )
 
+    batches = {4: LEVELS, 1: 4, 0: 1}
+
     def out_far(level, act):
-        pair = pl.ds(level, 2)
+        pair = pl.ds(level, batches[level] - level)
         to_columns(
             lambda g: xlow.at[pair, :, pl.ds(g * blk, blk)], landed.at[pair, c],
             out_s.at[level], out_r.at[level], act,
@@ -339,7 +341,7 @@
 
     def f_far(level, act):
         for step in range(1, nc):
-            to = (c + step) % nc
+            to = cols[step]
             copy = remote(
                 fpart.at[level, share(to), :], fsum.at[level, step - 1],
                 f_s.at[level, step], f_r.at[level], (z, to),
@@ -350,7 +352,7 @@
         here = xfull.at[level, share(c), :]
         for step in range(1, nc):
             copy = remote(
-                xlow.at[level], here, xf_s.at[level, step], xf_r.at[level], (z, (c + step) % nc)
+                xlow.at[level], here, xf_s.at[level, step], xf_r.at[level], (z, cols[step])
             )
             copy.start() if act else copy.wait_send()
         if act:
@@ -358,11 +360,11 @@
 
     def b_far(level, act):
         for step in range(nc):
-            to = (c + step) % nc
+            to = cols[step]
             src, dst = bpart.at[level, share(to), :], bsum.at[level, z, :, lane(mine, blk)]
 
             def go():
-                copy = remote(src, dst, b_s.at[level, step], b_r.at[level], (c % nz, to))
+                copy = remote(src, dst, b_s.at[level, step], b_r.at[level], (home, to))
                 copy.start() if act else copy.wait_send()
 
             if step > 0:
@@ -387,7 +389,7 @@
         return [
             apply(
                 value[:, g * blk : (g + 1) * blk],
-                diag[g, level, :, :blk], diag[g, level, :, blk:], dims,
+                diag[level, g, :, :blk], diag[level, g, :, blk:], dims,
             )
             for g in range(groups)
         ]
@@ -413,7 +415,7 @@
         solved = jnp.concatenate(solve(level, resid, NT), axis=1)
         yval[level] = solved
         if level < last:
-            ylow[level, :, lane(z, span)] = solved.astype(jnp.bfloat16)
+            ylow[level, :, lane(rank, span)] = solved.astype(jnp.bfloat16)
             for step in range(1, nz):
                 y_copy(level, step).start()
             if level < last - 1:
@@ -436,10 +438,9 @@
             relay(level + 1)
 
     def part_copy(level, step):
-        to = (z + step) % nz
         return remote(
-            part.at[level, :, lane(to, span)], sums.at[level, step - 1],
-            p_s.at[level, step], p_r.at[level, step], (to, c),
+            part.at[level, :, lane(ranks[step], span)], sums.at[level, step - 1],
+            p_s.at[level, step], p_r.at[level, step], (rows_z[step], c),
         )
 
     for level in reversed(range(LEVELS)):
@@ -459,11 +460,11 @@
                     value = term if value is None else value + term
                 bpart[level - 1] = value.astype(jnp.bfloat16)
                 b_far(level - 1, True)
-            if level % 2 == 1:
+            if level + 1 in batches:
                 out_far(level + 1, True)
         resid = yval[level]
         if level < last:
-            resid = resid - part[level, :, lane(z, span)].astype(jnp.float32)
+            resid = resid - part[level, :, lane(rank, span)].astype(jnp.float32)
         if level < last - 1:
             all_in(bsum.at[level], b_r.at[level])
             for step in range(nz):
@@ -494,10 +495,10 @@
             for step in range(1, nc):
                 load_copy(cut, step).wait_send()
 
-    for level in reversed(range(0, LEVELS, 2)):
+    for level, stop in batches.items():
         out_far(level, False)
-        all_in(landed.at[pl.ds(level, 2)], out_r.at[level])
-        out[level : level + 2] = landed[level : level + 2]
+        all_in(landed.at[pl.ds(level, stop - level)], out_r.at[level])
+        out[level:stop] = landed[level:stop]
 
 
 def split_plan(factor, pattern, loads, block_inverse):
@@ -521,7 +522,7 @@
             pltpu.VMEM((LEVELS, span, nc * blk), low),
             pltpu.VMEM((LEVELS, span, cols * blk), low),
             pltpu.VMEM((groups, LEVELS, width, blk), f32),
-            pltpu.VMEM((groups, LEVELS, blk, 2 * blk), low),
+            pltpu.VMEM((LEVELS, groups, blk, 2 * blk), low),
             pltpu.VMEM((LEVELS, width, span), f32),
             pltpu.VMEM((LEVELS, width, nc * blk), low),
             pltpu.VMEM((scen, LEVELS * blk), low),
@@ -534,11 +535,11 @@
             pltpu.VMEM((LEVELS, scen, blk), low),
             pltpu.VMEM((LEVELS, nz, width, span), low),
             pltpu.VMEM((LEVELS, nc, width, blk), low),
-            dma((LEVELS, chips)), dma((LEVELS, chips)),
+            dma((LEVELS,)), dma((LEVELS,)),
             dma((LEVELS, chips)), dma((LEVELS, chips)),
             dma((3,)), dma((3, nc)), dma((3, groups)),
             dma((LEVELS,)), dma((LEVELS, chips)), dma((LEVELS, groups)),
-            dma((LEVELS, groups)), dma((LEVELS, groups)),
+            dma((LEVELS,)), dma((LEVELS,)),
             dma((LEVELS, nz)), dma((LEVELS, nz)),
             dma((LEVELS, nz, groups)), dma((LEVELS,)),
             dma((LEVELS, nc)), dma((LEVELS,)),

time: 127 us -> 123 us (0.969)
  Pallas kernels: 124 us -> 119 us
    pallas_call x1, Pallas kernels: 124 us -> 119 us  [split_plan(): pl.pallas_call(functools.partial(kernel, nz, nc, blk, scen), out_shape=ja...]
where the time goes in v6:
time: 123 us; the launch traced here: 122 us
  Pallas kernels  119 us (97%)
  local copies, waits for them, and re-layouts  3.11 us (3%)
    pallas_call x1, Pallas kernels, split_plan(): pl.pallas_call(functools.partial(kernel, nz, nc, blk, scen), out_shape=ja...  119 us

profile of v6, /device:TPU:0, one launch (start us, length us, event | category | flops | bytes accessed | tf_op | source)
XLA Modules:
  0.0 122.4 jit_solution(12724911005442518688)
XLA Ops:
  0.0 0.8 copy.5.pattern
  0.8 0.0 copy-start
  0.8 1.0 copy-done
  1.8 119.1 %shard_map.46 = bf16[8,8,32,128]{3,2,1,0:T(8,128)(2,1)S(1)} custom-call(bf16[16,8,128,128]{3,2,1,0:T(8,128)(2,1)} %bitcast.11, s32[16,8]{1,0:T(8,128)S(1)} %copy.5.pattern, f32[8,128,256]{2,1,0:T(8,128)} %bitcast.12, f32[8,128,128]{2,1,0:T(8,128)S(1)} %bitcast.10), custom_call_target="tpu_custom_call" | custom-call | tf_op jit(solution)/shard_map/pallas_call | solution.py:514
  120.9 0.1 bitcast_convert_fusion
  121.1 1.3 %copy.6 = f32[8,256,128]{1,2,0:T(8,128)} copy(f32[8,256,128]{2,1,0:T(8,128)S(1)} %bitcast_convert_fusion) | data formatting | bytes 2097152 | tf_op jit(solution)/shard_map/broadcast_in_dim | solution.py:556
Async XLA Ops:
  0.8 1.0 copy-start

commit v7 on v6

--- a/solution.py
+++ b/solution.py
@@ -300,17 +300,17 @@
     def y_copy(level, step):
         here = ylow.at[level, :, lane(rank, span)]
         return remote(
-            here, here, y_s.at[level, step], y_r.at[level, step], (rows_z[step], c)
-        )
-
-    def to_columns(source, dst, s, r, act):
+            here, here, y_s.at[level], y_r.at[level, step], (rows_z[step], c)
+        )
+
+    def to_columns(source, dst, s, r, act, single):
         for g in range(groups):
             src = source(g)
 
             for step in range(nz):
                 def go():
                     copy = remote(
-                        src, dst, s.at[step, g], r, (rows_z[step], z + nz * g)
+                        src, dst, s if single else s.at[step, g], r, (rows_z[step], z + nz * g)
                     )
                     copy.start() if act else copy.wait_send()
 
@@ -327,7 +327,7 @@
         to_columns(
             lambda g: ylow.at[level, :, lane(rank * groups + g, blk)],
             yfull.at[share(c), pl.ds(level * blk, blk)],
-            yf_s.at[level], yf_r.at[level], act,
+            yf_s.at[level], yf_r.at[level], act, True,
         )
 
     batches = {4: LEVELS, 1: 4, 0: 1}
@@ -336,7 +336,7 @@
         pair = pl.ds(level, batches[level] - level)
         to_columns(
             lambda g: xlow.at[pair, :, pl.ds(g * blk, blk)], landed.at[pair, c],
-            out_s.at[level], out_r.at[level], act,
+            out_s.at[level], out_r.at[level], act, False,
         )
 
     def f_far(level, act):
@@ -344,7 +344,7 @@
             to = cols[step]
             copy = remote(
                 fpart.at[level, share(to), :], fsum.at[level, step - 1],
-                f_s.at[level, step], f_r.at[level], (z, to),
+                f_s.at[level], f_r.at[level], (z, to),
             )
             copy.start() if act else copy.wait_send()
 
@@ -352,7 +352,7 @@
         here = xfull.at[level, share(c), :]
         for step in range(1, nc):
             copy = remote(
-                xlow.at[level], here, xf_s.at[level, step], xf_r.at[level], (z, cols[step])
+                xlow.at[level], here, xf_s.at[level], xf_r.at[level], (z, cols[step])
             )
             copy.start() if act else copy.wait_send()
         if act:
@@ -364,7 +364,7 @@
             src, dst = bpart.at[level, share(to), :], bsum.at[level, z, :, lane(mine, blk)]
 
             def go():
-                copy = remote(src, dst, b_s.at[level, step], b_r.at[level], (home, to))
+                copy = remote(src, dst, b_s.at[level], b_r.at[level], (home, to))
                 copy.start() if act else copy.wait_send()
 
             if step > 0:
@@ -440,7 +440,7 @@
     def part_copy(level, step):
         return remote(
             part.at[level, :, lane(ranks[step], span)], sums.at[level, step - 1],
-            p_s.at[level, step], p_r.at[level, step], (rows_z[step], c),
+            p_s.at[level], p_r.at[level, step], (rows_z[step], c),
         )
 
     for level in reversed(range(LEVELS)):
@@ -478,14 +478,24 @@
 
     out_far(0, True)
     for level in range(last):
-        for step in range(1, nz):
-            y_copy(level, step).wait_send()
-            part_copy(level, step).wait_send()
+        all_in(sums.at[level], y_s.at[level])
+        all_in(sums.at[level], p_s.at[level])
         if level < last - 1:
-            y_far(level, False)
-            b_far(level, False)
-            f_far(level + 2, False)
-            x_far(level + 2, False)
+            all_in(fsum.at[level + 2], f_s.at[level + 2])
+            all_in(fsum.at[level + 2], xf_s.at[level + 2])
+
+    @pl.when(owner)
+    def _():
+        for level in range(last - 1):
+            all_in(landed.at[level, pl.ds(0, nc - 1)], yf_s.at[level])
+            all_in(landed.at[level, pl.ds(0, nc - 1)], b_s.at[level])
+
+    @pl.when(jnp.logical_not(owner))
+    def _():
+        for level in range(last - 1):
+            all_in(landed.at[level], yf_s.at[level])
+            all_in(landed.at[level], b_s.at[level])
+
     for level in range(LEVELS):
         spread_sent(level)
 
@@ -540,12 +550,12 @@
             dma((3,)), dma((3, nc)), dma((3, groups)),
             dma((LEVELS,)), dma((LEVELS, chips)), dma((LEVELS, groups)),
             dma((LEVELS,)), dma((LEVELS,)),
-            dma((LEVELS, nz)), dma((LEVELS, nz)),
-            dma((LEVELS, nz, groups)), dma((LEVELS,)),
-            dma((LEVELS, nc)), dma((LEVELS,)),
-            dma((LEVELS, nz)), dma((LEVELS, nz)),
-            dma((LEVELS, nc)), dma((LEVELS,)),
-            dma((LEVELS, nc)), dma((LEVELS,)),
+            dma((LEVELS,)), dma((LEVELS, nz)),
+            dma((LEVELS,)), dma((LEVELS,)),
+            dma((LEVELS,)), dma((LEVELS,)),
+            dma((LEVELS,)), dma((LEVELS, nz)),
+            dma((LEVELS,)), dma((LEVELS,)),
+            dma((LEVELS,)), dma((LEVELS,)),
             dma((LEVELS, nz, groups)), dma((LEVELS,)),
         ],
         compiler_params=pltpu.CompilerParams(

time: 123 us -> 121 us (0.984)
  Pallas kernels: 119 us -> 117 us
    pallas_call x1, Pallas kernels: 119 us -> 117 us  [split_plan(): pl.pallas_call(functools.partial(kernel, nz, nc, blk, scen), out_shape=ja...]
where the time goes in v7:
time: 121 us; the launch traced here: 120 us
  Pallas kernels  117 us (97%)
  local copies, waits for them, and re-layouts  3.11 us (3%)
    pallas_call x1, Pallas kernels, split_plan(): pl.pallas_call(functools.partial(kernel, nz, nc, blk, scen), out_shape=ja...  117 us

profile of v7, /device:TPU:0, one launch (start us, length us, event | category | flops | bytes accessed | tf_op | source)
XLA Modules:
  0.0 120.0 jit_solution(2784442020167947998)
XLA Ops:
  0.0 0.8 copy.5.pattern
  0.8 0.0 copy-start
  0.8 1.0 copy-done
  1.8 116.8 %shard_map.46 = bf16[8,8,32,128]{3,2,1,0:T(8,128)(2,1)S(1)} custom-call(bf16[16,8,128,128]{3,2,1,0:T(8,128)(2,1)} %bitcast.11, s32[16,8]{1,0:T(8,128)S(1)} %copy.5.pattern, f32[8,128,256]{2,1,0:T(8,128)} %bitcast.12, f32[8,128,128]{2,1,0:T(8,128)S(1)} %bitcast.10), custom_call_target="tpu_custom_call" | custom-call | tf_op jit(solution)/shard_map/pallas_call | solution.py:524
  118.6 0.1 bitcast_convert_fusion
  118.7 1.3 %copy.6 = f32[8,256,128]{1,2,0:T(8,128)} copy(f32[8,256,128]{2,1,0:T(8,128)S(1)} %bitcast_convert_fusion) | data formatting | bytes 2097152 | tf_op jit(solution)/shard_map/broadcast_in_dim | solution.py:566
Async XLA Ops:
  0.8 1.0 copy-start
